TPU v7x, 32 devices: a whole 2x2x4 slice. The times are simulated.
32 devices in a mesh: dp: 8 (over z, x), mp: 4 (over y, core).
Axes of the slice: x: 2, y: 2, z: 4, core: 2. Of those that a mesh axis runs over, the one named last changes fastest.
Arguments:
- block_input: bfloat16 [24576, 1024], P(('dp', 'mp')), may hold values from -6 to 6
- sequence_lengths: int32 [8, 6], P('dp'), may hold values from 0 to 1024, as said below
- first_gain: float32 [1024], replicated, may hold values from 0.5 to 1.5
- first_shift: float32 [1024], replicated, may hold values from -3 to 3
- second_gain: float32 [1024], replicated, may hold values from 0.5 to 1.5
- second_shift: float32 [1024], replicated, may hold values from -3 to 3
- triple_weight: bfloat16 [1024, 3072], P(None, 'mp'), may hold values from -0.1875 to 0.1875
- triple_left: bfloat16 [1024, 128], replicated, may hold values from -0.1875 to 0.1875
- triple_right: bfloat16 [128, 3072], replicated, may hold values from -0.25 to 0.25
- output_weight: bfloat16 [1024, 1024], P('mp'), may hold values from -0.5 to 0.5
- output_left: bfloat16 [1024, 128], replicated, may hold values from -0.5 to 0.5
- output_right: bfloat16 [128, 1024], replicated, may hold values from -0.25 to 0.25
- expand_weight: bfloat16 [1024, 4096], P(None, 'mp'), may hold values from -0.1875 to 0.1875
- expand_left: bfloat16 [1024, 128], replicated, may hold values from -0.1875 to 0.1875
- expand_right: bfloat16 [128, 4096], replicated, may hold values from -0.25 to 0.25
- shrink_weight: bfloat16 [4096, 1024], P('mp'), may hold values from -0.09375 to 0.09375
- shrink_left: bfloat16 [4096, 128], replicated, may hold values from -0.09375 to 0.09375
- shrink_right: bfloat16 [128, 1024], replicated, may hold values from -0.25 to 0.25
- cotangent: bfloat16 [24576, 1024], P(('dp', 'mp')), may hold values from -6 to 6
Outputs:
- block_output: bfloat16 [24576, 1024], P(('dp', 'mp'))
- input_gradient: float32 [24576, 1024], P(('dp', 'mp'))
- first_gain_gradient: float32 [1024], replicated
- first_shift_gradient: float32 [1024], replicated
- second_gain_gradient: float32 [1024], replicated
- second_shift_gradient: float32 [1024], replicated
- triple_left_gradient: float32 [1024, 128], replicated
- triple_right_gradient: float32 [128, 3072], replicated
- output_left_gradient: float32 [1024, 128], replicated
- output_right_gradient: float32 [128, 1024], replicated
- expand_left_gradient: float32 [1024, 128], replicated
- expand_right_gradient: float32 [128, 4096], replicated
- shrink_left_gradient: float32 [4096, 128], replicated
- shrink_right_gradient: float32 [128, 1024], replicated
Inputs may be any that keep to these rules, and one draw needn't show every extreme that they name: `sequence_lengths`: row g lists the lengths of the sequences of group g in order, each 512 or 1024, then zeros; every row sums to 3072 and holds at least one sequence of 1024.
All inputs are finite; a program needn't handle non-finite values.
Results may differ from a plain program's by a relative error of at most 0.012.
The roundings to bfloat16 on the way count: a program that leaves them out, or rounds other values in their place, can miss the bound.
Values may be sent and summed in bfloat16 or wider, within the bound.
A program may use at most 256 MiB of HBM per device.

v0:
```python
import math

import jax
import jax.numpy as jnp
from jax import lax
from jax.sharding import PartitionSpec as P

HEAD_DIM = 64
ROT = 16
SHORT = 512
TOK_GRP = 3072
SLOTS = 6


EPS = 1e-05


def dot_plain(former, latter):
    return jnp.dot(former, latter, preferred_element_type=jnp.float32)


def dot_lead(former, latter):
    return lax.dot_general(
        former, latter, (((0,), (0,)), ((), ())), preferred_element_type=jnp.float32
    )


def dot_tail(former, latter):
    return lax.dot_general(
        former, latter, (((1,), (1,)), ((), ())), preferred_element_type=jnp.float32
    )


def split_parts(values):
    upper = values.astype(jnp.bfloat16)
    lower = (values - upper.astype(jnp.float32)).astype(jnp.bfloat16)
    return (upper, lower)


def lead_exact(narrow, wide_values):
    upper, lower = split_parts(wide_values)
    return dot_lead(narrow, upper) + dot_lead(narrow, lower)


def tail_exact(wide_values, narrow):
    upper, lower = split_parts(wide_values)
    return dot_tail(upper, narrow) + dot_tail(lower, narrow)


def layer_norm(values, norm_gain, norm_shift):
    center = values - jnp.mean(values, axis=-1, keepdims=True)
    spread = jnp.mean(center * center, axis=-1, keepdims=True)
    return center * lax.rsqrt(spread + EPS) * norm_gain + norm_shift


def norm_pair(values, first_gain, first_shift, second_gain, second_shift):
    return (
        layer_norm(values, first_gain, first_shift),
        layer_norm(values, second_gain, second_shift),
    )


def find_flags(group_lengths):
    seq_ends = jnp.cumsum(group_lengths, dtype=jnp.int32)
    starts = seq_ends - group_lengths
    block_starts = jnp.arange(SLOTS, dtype=jnp.int32) * SHORT
    begins = jnp.any(
        (starts[None, :] == block_starts[:, None]) & (group_lengths[None, :] > 0), axis=1
    )
    return jnp.where(begins, 0, 1).astype(jnp.int32)


def rotary_tables(continues):
    row_index = jnp.arange(TOK_GRP, dtype=jnp.int32)
    positions = row_index % SHORT + SHORT * jnp.repeat(continues, SHORT)
    half_rot = ROT // 2
    frequency = jnp.exp(jnp.arange(half_rot, dtype=jnp.float32) * (-2.0 * math.log(10000.0) / ROT))
    angles = positions.astype(jnp.float32)[:, None] * frequency[None, :]
    return (jnp.cos(angles)[:, None, :], jnp.sin(angles)[:, None, :])


def rotate(head_rows, cosine, sine_table):
    half_rot = ROT // 2
    first_half = head_rows[:, :, :half_rot]
    second_half = head_rows[:, :, half_rot:ROT]
    return jnp.concatenate(
        [
            first_half * cosine - second_half * sine_table,
            second_half * cosine + first_half * sine_table,
            head_rows[:, :, ROT:],
        ],
        axis=2,
    )


def unrotate(head_grads, cosine, sine_table):
    half_rot = ROT // 2
    first_half = head_grads[:, :, :half_rot]
    second_half = head_grads[:, :, half_rot:ROT]
    return jnp.concatenate(
        [
            first_half * cosine + second_half * sine_table,
            second_half * cosine - first_half * sine_table,
            head_grads[:, :, ROT:],
        ],
        axis=2,
    )


def causal_mask(continued):
    query_index = jnp.arange(SHORT, dtype=jnp.int32)[:, None]
    key_index = jnp.arange(2 * SHORT, dtype=jnp.int32)[None, :]
    return jnp.where(key_index < SHORT, continued > 0, key_index - SHORT <= query_index)


def key_windows(key_rows):
    padded = jnp.concatenate(
        [jnp.zeros((SHORT,) + key_rows.shape[1:], key_rows.dtype), key_rows], axis=0
    )
    blocks = padded.reshape((SLOTS + 1, SHORT) + key_rows.shape[1:])
    return jnp.concatenate([blocks[:-1], blocks[1:]], axis=1)


def masked_scores(query_blk, key_win, continued):
    scores = jnp.einsum(
        "qhd,khd->hqk", query_blk, key_win, preferred_element_type=jnp.float32
    ) * HEAD_DIM ** (-0.5)
    return jnp.where(causal_mask(continued)[None], scores, -1e30)


def attend_forward(queries, key_rows, value_rows, continues):

    def one_block(block_items):
        query_blk, key_win, value_win, continued = block_items
        scores = masked_scores(query_blk, key_win, continued)
        row_peak = jnp.max(scores, axis=-1, keepdims=True)
        exp_scores = jnp.exp(scores - row_peak)
        row_total = jnp.sum(exp_scores, axis=-1, keepdims=True)
        weights_low = (exp_scores / row_total).astype(jnp.bfloat16)
        attended = jnp.einsum(
            "hqk,khd->qhd", weights_low, value_win, preferred_element_type=jnp.float32
        )
        return (attended, row_peak + jnp.log(row_total))

    query_blocks = queries.reshape((SLOTS, SHORT) + queries.shape[1:])
    attended, log_totals = lax.map(
        one_block, (query_blocks, key_windows(key_rows), key_windows(value_rows), continues)
    )
    return (attended.reshape(queries.shape), log_totals)


def fold_windows(window_grads, full_shape):
    own_part = window_grads[:, SHORT:]
    later_part = jnp.concatenate(
        [window_grads[1:, :SHORT], jnp.zeros_like(window_grads[:1, :SHORT])], axis=0
    )
    return (own_part + later_part).reshape(full_shape)


def attend_backward(queries, key_rows, value_rows, continues, log_totals, grad_out):
    score_scale = HEAD_DIM ** (-0.5)

    def one_block(block_items):
        query_blk, key_win, value_win, continued, log_total, grad_blk = block_items
        scores = masked_scores(query_blk, key_win, continued)
        weights_full = jnp.exp(scores - log_total)
        weights_low = weights_full.astype(jnp.bfloat16)
        grad_weights = jnp.einsum(
            "qhd,khd->hqk", grad_blk, value_win, preferred_element_type=jnp.float32
        )
        grad_values = jnp.einsum(
            "hqk,qhd->khd", weights_low, grad_blk, preferred_element_type=jnp.float32
        )
        row_inner = jnp.sum(weights_full * grad_weights, axis=-1, keepdims=True)
        grad_scores = (weights_full * (grad_weights - row_inner)).astype(jnp.bfloat16)
        grad_query = (
            jnp.einsum("hqk,khd->qhd", grad_scores, key_win, preferred_element_type=jnp.float32)
            * score_scale
        )
        grad_keys = (
            jnp.einsum("hqk,qhd->khd", grad_scores, query_blk, preferred_element_type=jnp.float32)
            * score_scale
        )
        return (grad_query, grad_keys, grad_values)

    block_shape = (SLOTS, SHORT) + queries.shape[1:]
    grad_query, grad_keys, grad_values = lax.map(
        one_block,
        (
            queries.reshape(block_shape),
            key_windows(key_rows),
            key_windows(value_rows),
            continues,
            log_totals,
            grad_out.reshape(block_shape),
        ),
    )
    return (
        grad_query.reshape(queries.shape),
        fold_windows(grad_keys, queries.shape),
        fold_windows(grad_values, queries.shape),
    )


def place_rows(piece_rows, total_rows, start):
    return lax.dynamic_update_slice_in_dim(
        jnp.zeros((total_rows, piece_rows.shape[1]), jnp.float32), piece_rows, start, 0
    )


def place_cols(piece_cols, total_cols, start):
    return lax.dynamic_update_slice_in_dim(
        jnp.zeros((piece_cols.shape[0], total_cols), jnp.float32), piece_cols, start, 1
    )


def shards(
    block_input,
    sequence_lengths,
    first_gain,
    first_shift,
    second_gain,
    second_shift,
    triple_weight,
    triple_left,
    triple_right,
    output_weight,
    output_left,
    output_right,
    expand_weight,
    expand_left,
    expand_right,
    shrink_weight,
    shrink_left,
    shrink_right,
    cotangent,
):
    rank_index = lax.axis_index("mp")
    triple_width = triple_weight.shape[1]
    head_count = triple_width // (3 * HEAD_DIM)
    feature_width = output_weight.shape[0]
    hidden_width = expand_weight.shape[1]
    own_input = block_input.astype(jnp.float32)
    continues = find_flags(sequence_lengths[0])
    cosine, sine_table = rotary_tables(continues)
    normed_first, normed_second = norm_pair(
        own_input, first_gain, first_shift, second_gain, second_shift
    )
    full_first, full_second = (
        lax.all_gather(normed_first.astype(jnp.bfloat16), "mp", axis=0, tiled=True),
        lax.all_gather(normed_second.astype(jnp.bfloat16), "mp", axis=0, tiled=True),
    )
    row_count = full_first.shape[0]
    triple_cols = lax.dynamic_slice_in_dim(triple_right, rank_index * triple_width, triple_width, 1)
    expand_cols = lax.dynamic_slice_in_dim(expand_right, rank_index * hidden_width, hidden_width, 1)
    output_rows = lax.dynamic_slice_in_dim(
        output_left, rank_index * feature_width, feature_width, 0
    )
    shrink_rows = lax.dynamic_slice_in_dim(shrink_left, rank_index * hidden_width, hidden_width, 0)
    low_first = dot_plain(full_first, triple_left).astype(jnp.bfloat16)
    mixed = dot_plain(full_first, triple_weight) + dot_plain(low_first, triple_cols)
    mixed = mixed.reshape(row_count, head_count, 3, HEAD_DIM)
    queries = rotate(mixed[:, :, 0], cosine, sine_table).astype(jnp.bfloat16)
    key_rows = rotate(mixed[:, :, 1], cosine, sine_table).astype(jnp.bfloat16)
    value_rows = mixed[:, :, 2].astype(jnp.bfloat16)
    attended, log_totals = attend_forward(queries, key_rows, value_rows, continues)
    attended_low = attended.reshape(row_count, feature_width).astype(jnp.bfloat16)
    low_second = dot_plain(full_second, expand_left).astype(jnp.bfloat16)
    hidden_pre = dot_plain(full_second, expand_weight) + dot_plain(low_second, expand_cols)
    activated = jax.nn.gelu(hidden_pre, approximate=False).astype(jnp.bfloat16)
    partial_out = dot_plain(attended_low, output_weight) + dot_plain(activated, shrink_weight)
    partial_attended = dot_plain(attended_low, output_rows)
    partial_activated = dot_plain(activated, shrink_rows)
    summed_out, summed_attended, summed_activated = (
        lax.psum_scatter(partial_out, "mp", scatter_dimension=0, tiled=True),
        lax.psum_scatter(partial_attended, "mp", scatter_dimension=0, tiled=True),
        lax.psum_scatter(partial_activated, "mp", scatter_dimension=0, tiled=True),
    )
    low_attended = summed_attended.astype(jnp.bfloat16)
    low_activated = summed_activated.astype(jnp.bfloat16)
    block_output = (
        own_input
        + summed_out
        + dot_plain(low_attended, output_right)
        + dot_plain(low_activated, shrink_right)
    ).astype(jnp.bfloat16)
    grad_own = cotangent.astype(jnp.float32)
    grad_low_attended = dot_tail(cotangent, output_right).astype(jnp.bfloat16)
    grad_low_activated = dot_tail(cotangent, shrink_right).astype(jnp.bfloat16)
    output_right_grad = dot_lead(low_attended, cotangent)
    shrink_right_grad = dot_lead(low_activated, cotangent)
    full_grad, full_grad_attended, full_grad_activated = (
        lax.all_gather(cotangent, "mp", axis=0, tiled=True),
        lax.all_gather(grad_low_attended, "mp", axis=0, tiled=True),
        lax.all_gather(grad_low_activated, "mp", axis=0, tiled=True),
    )
    grad_attended = dot_tail(full_grad, output_weight) + dot_tail(full_grad_attended, output_rows)
    grad_attended = grad_attended.astype(jnp.bfloat16).reshape(row_count, head_count, HEAD_DIM)
    output_left_part = dot_lead(attended_low, full_grad_attended)
    grad_activated = dot_tail(full_grad, shrink_weight) + dot_tail(full_grad_activated, shrink_rows)
    shrink_left_part = dot_lead(activated, full_grad_activated)
    gelu_pull = jax.vjp(lambda values: jax.nn.gelu(values, approximate=False), hidden_pre)[1]
    grad_hidden = gelu_pull(grad_activated)[0].astype(jnp.bfloat16)
    expand_right_part = dot_lead(low_second, grad_hidden)
    grad_low_second = dot_tail(grad_hidden, expand_cols)
    expand_left_grad = lead_exact(full_second, grad_low_second)
    grad_second = dot_tail(grad_hidden, expand_weight) + tail_exact(grad_low_second, expand_left)
    grad_query, grad_keys, grad_values = attend_backward(
        queries, key_rows, value_rows, continues, log_totals, grad_attended
    )
    grad_query = unrotate(grad_query, cosine, sine_table)
    grad_keys = unrotate(grad_keys, cosine, sine_table)
    grad_mixed = (
        jnp.stack([grad_query, grad_keys, grad_values], axis=2)
        .reshape(row_count, triple_width)
        .astype(jnp.bfloat16)
    )
    triple_right_part = dot_lead(low_first, grad_mixed)
    grad_low_first = dot_tail(grad_mixed, triple_cols)
    triple_left_grad = lead_exact(full_first, grad_low_first)
    grad_first = dot_tail(grad_mixed, triple_weight) + tail_exact(grad_low_first, triple_left)
    sum_first, sum_second = (
        lax.psum_scatter(
            grad_first.astype(jnp.bfloat16), "mp", scatter_dimension=0, tiled=True
        ).astype(jnp.float32),
        lax.psum_scatter(
            grad_second.astype(jnp.bfloat16), "mp", scatter_dimension=0, tiled=True
        ).astype(jnp.float32),
    )
    norm_pull = jax.vjp(norm_pair, own_input, first_gain, first_shift, second_gain, second_shift)[1]
    norm_grads = norm_pull((sum_first, sum_second))
    input_gradient = grad_own + norm_grads[0]
    totals = lax.psum(
        (
            norm_grads[1],
            norm_grads[2],
            norm_grads[3],
            norm_grads[4],
            triple_left_grad,
            place_cols(triple_right_part, triple_right.shape[1], rank_index * triple_width),
            place_rows(output_left_part, output_left.shape[0], rank_index * feature_width),
            output_right_grad,
            expand_left_grad,
            place_cols(expand_right_part, expand_right.shape[1], rank_index * hidden_width),
            place_rows(shrink_left_part, shrink_left.shape[0], rank_index * hidden_width),
            shrink_right_grad,
        ),
        ("dp", "mp"),
    )
    return (
        block_output,
        input_gradient,
        totals[0],
        totals[1],
        totals[2],
        totals[3],
        totals[4],
        totals[5],
        totals[6],
        totals[7],
        totals[8],
        totals[9],
        totals[10],
        totals[11],
    )


def solution(mesh):
    placed = (
        P(("dp", "mp"), None),
        P("dp", None),
        P(),
        P(),
        P(),
        P(),
        P(None, "mp"),
        P(),
        P(),
        P("mp", None),
        P(),
        P(),
        P(None, "mp"),
        P(),
        P(),
        P("mp", None),
        P(),
        P(),
        P(("dp", "mp"), None),
    )
    return jax.shard_map(
        shards,
        mesh=mesh,
        in_specs=placed,
        out_specs=(
            P(("dp", "mp"), None),
            P(("dp", "mp"), None),
            P(),
            P(),
            P(),
            P(),
            P(),
            P(),
            P(),
            P(),
            P(),
            P(),
            P(),
            P(),
        ),
        check_vma=False,
    )
```

profile of v0, /device:TPU:1, one launch (start us, length us, event | category | flops | bytes accessed | tf_op | source)
XLA Modules:
  0.0 1003.0 jit_solution(11942274259815254138)
XLA Ops:
  18.5 10.7 %all_gather.19 = bf16[3072,128]{1,0:T(8,128)(2,1)} all-gather(bf16[768,128]{1,0:T(8,128)(2,1)S(1)} %convolution_convert_fusion.2), channel_id=1, replica_groups=mesh['dp'=8,'mp'=4] {'mp'}, dimensions={0}, use_global_device_ids=true | all-gather | bytes 983040 | tf_op jit(solution)/shard_map/all_gather | solution.py:294
  30.2 33.2 %all-gather.4.cloned.1.call-done = bf16[3072,1024]{1,0:T(8,128)(2,1)} async-done(((bf16[768,1024]{1,0:T(8,128)(2,1)}), bf16[3072,1024]{1,0:T(8,128)(2,1)}) %all-gather.4.cloned.1.call-update) | async-done | bytes 6291472 | tf_op jit(solution)/shard_map/all_gather | solution.py:250
  135.2 70.5 %while.30 = (s32[]{:T(128)}, bf16[6,512,4,64]{1,3,2,0:T(8,128)(2,1)}, f32[6,4,512,1]{2,1,3,0:T(4,128)}, bf16[6,1024,4,64]{1,3,2,0:T(8,128)(2,1)}, s32[6]{0:T(128...) while((s32[]{:T(128)}, ...), condition=%wide.region_7.8_spmd, body=%wide.region_4.7_spmd.sunk | while | flops 563085312 | bytes 29176436 | solution.py:146
  224.4 216.4 %while.31 = (s32[]{:T(128)}, f32[6,512,4,64]{1,0,3,2:T(8,128)}, f32[6,1024,4,64]{1,3,2,0:T(8,128)}, f32[6,1024,4,64]{1,3,2,0:T(8,128)}, bf16[6,1024,4,64]{1,3,2,...) while((s32[]{:T(128)}, f32[6,512,4,64]{1,0,3,2:T(8,128)}, ...), condition=%wide.region_16.17_spmd, body=%wide.region_14.16_spmd.sunk | while | flops 1375076352 | bytes 105978552 | solution.py:187
  242.3 11.5 %dynamic_update_slice.66 = f32[6,512,4,64]{1,0,3,2:T(8,128)} dynamic-update-slice(f32[6,512,4,64]{1,0,3,2:T(8,128)} %get-tuple-element.520, f32[1,512,4,64]{1,0,3,2:T(1,128)S(1)} %copy.89, s32[]{:T(128)} %get-tuple-element.519, s32[]{:T(128)} %constant.187.clone.1..sunk, s32[]{:T(128)} %constant.187.clone.1..sunk, s32[]{:T(128)} %constant.187.clone.1..sunk) | dynamic-update-slice | bytes 1048580 | tf_op jit(solution)/shard_map/while/body/jit(dynamic_update_index_in_dim)/dynamic_update_slice | solution.py:146
  278.2 11.5 %dynamic_update_slice.66 = f32[6,512,4,64]{1,0,3,2:T(8,128)} dynamic-update-slice(f32[6,512,4,64]{1,0,3,2:T(8,128)} %get-tuple-element.520, f32[1,512,4,64]{1,0,3,2:T(1,128)S(1)} %copy.89, s32[]{:T(128)} %get-tuple-element.519, s32[]{:T(128)} %constant.187.clone.1..sunk, s32[]{:T(128)} %constant.187.clone.1..sunk, s32[]{:T(128)} %constant.187.clone.1..sunk) | dynamic-update-slice | bytes 1048580 | tf_op jit(solution)/shard_map/while/body/jit(dynamic_update_index_in_dim)/dynamic_update_slice | solution.py:146
  314.2 11.5 %dynamic_update_slice.66 = f32[6,512,4,64]{1,0,3,2:T(8,128)} dynamic-update-slice(f32[6,512,4,64]{1,0,3,2:T(8,128)} %get-tuple-element.520, f32[1,512,4,64]{1,0,3,2:T(1,128)S(1)} %copy.89, s32[]{:T(128)} %get-tuple-element.519, s32[]{:T(128)} %constant.187.clone.1..sunk, s32[]{:T(128)} %constant.187.clone.1..sunk, s32[]{:T(128)} %constant.187.clone.1..sunk) | dynamic-update-slice | bytes 1048580 | tf_op jit(solution)/shard_map/while/body/jit(dynamic_update_index_in_dim)/dynamic_update_slice | solution.py:146
  350.3 11.5 %dynamic_update_slice.66 = f32[6,512,4,64]{1,0,3,2:T(8,128)} dynamic-update-slice(f32[6,512,4,64]{1,0,3,2:T(8,128)} %get-tuple-element.520, f32[1,512,4,64]{1,0,3,2:T(1,128)S(1)} %copy.89, s32[]{:T(128)} %get-tuple-element.519, s32[]{:T(128)} %constant.187.clone.1..sunk, s32[]{:T(128)} %constant.187.clone.1..sunk, s32[]{:T(128)} %constant.187.clone.1..sunk) | dynamic-update-slice | bytes 1048580 | tf_op jit(solution)/shard_map/while/body/jit(dynamic_update_index_in_dim)/dynamic_update_slice | solution.py:146
  386.2 11.5 %dynamic_update_slice.66 = f32[6,512,4,64]{1,0,3,2:T(8,128)} dynamic-update-slice(f32[6,512,4,64]{1,0,3,2:T(8,128)} %get-tuple-element.520, f32[1,512,4,64]{1,0,3,2:T(1,128)S(1)} %copy.89, s32[]{:T(128)} %get-tuple-element.519, s32[]{:T(128)} %constant.187.clone.1..sunk, s32[]{:T(128)} %constant.187.clone.1..sunk, s32[]{:T(128)} %constant.187.clone.1..sunk) | dynamic-update-slice | bytes 1048580 | tf_op jit(solution)/shard_map/while/body/jit(dynamic_update_index_in_dim)/dynamic_update_slice | solution.py:146
  397.7 6.8 fusion.230
  422.2 11.5 %dynamic_update_slice.66 = f32[6,512,4,64]{1,0,3,2:T(8,128)} dynamic-update-slice(f32[6,512,4,64]{1,0,3,2:T(8,128)} %get-tuple-element.520, f32[1,512,4,64]{1,0,3,2:T(1,128)S(1)} %copy.89, s32[]{:T(128)} %get-tuple-element.519, s32[]{:T(128)} %constant.187.clone.1..sunk, s32[]{:T(128)} %constant.187.clone.1..sunk, s32[]{:T(128)} %constant.187.clone.1..sunk) | dynamic-update-slice | bytes 1048580 | tf_op jit(solution)/shard_map/while/body/jit(dynamic_update_index_in_dim)/dynamic_update_slice | solution.py:146
  462.8 32.3 %multiply_convert_fusion.1 = (bf16[3072,1024]{1,0:T(8,128)(2,1)}, f32[3072,1024]{1,0:T(8,128)}, f32[3072,1024]{1,0:T(8,128)}) fusion(f32[3072,1024]{1,0:T(8,128)S(1)} %fusion.135, bf16[3072,128]{1,0:T(8,128)(2,1)S(1)} %convolution_convert_fusion, bf16[128,4096]{1,0:T(8,128)(2,1)} %param.37, s32[]{:T(128)S(6)} %select_n.66), kind=kOutput, calls=%fused_computation.70 | convolution fusion | flops 1012924416 | bytes 45088772 | tf_op jit(solution)/shard_map/dot_general | solution.py:19
  529.9 8.2 fusion.126
  538.0 10.7 %fusion.140 = f32[3072,1024]{1,0:T(8,128)} fusion(bf16[3072,768]{0,1:T(8,128)(2,1)} %bitcast.220, bf16[1024,768]{1,0:T(8,128)(2,1)S(1)} %copy-done.70), kind=kOutput, calls=%fused_computation.234 | convolution fusion | flops 4831838208 | bytes 18874368 | tf_op jit(solution)/shard_map/dot_general | solution.py:29
  548.8 12.1 %add_convert_fusion = bf16[3072,1024]{1,0:T(8,128)(2,1)} fusion(f32[3072,1024]{1,0:T(8,128)} %fusion.140, f32[3072,1024]{1,0:T(8,128)} %fusion.126, bf16[1024,128]{1,0:T(8,128)(2,1)S(1)} %copy-done.36, f32[3072,128]{1,0:T(8,128)S(1)} %copy-done.4), kind=kOutput, calls=%fused_computation.67 | convolution fusion | flops 816316416 | bytes 33292288 | tf_op jit(solution)/shard_map/dot_general | solution.py:29
  563.8 8.8 all_gather.18
  572.6 13.6 %fusion.137 = f32[3072,1024]{1,0:T(8,128)} fusion(bf16[3072,1024]{1,0:T(8,128)(2,1)} %all-gather.8.cloned.1.call-done, bf16[1024,1024]{1,0:T(8,128)(2,1)} %param.38), kind=kOutput, calls=%fused_computation.231 | convolution fusion | flops 6442450944 | bytes 20971520 | tf_op jit(solution)/shard_map/dot_general | solution.py:29
  586.2 16.8 %add_convert_fusion.2 = bf16[3072,1024]{1,0:T(8,128)(2,1)} fusion(f32[3072,1024]{1,0:T(8,128)} %get-tuple-element.337, f32[3072,1024]{1,0:T(8,128)} %fusion.137, f32[3072,1024]{1,0:T(8,128)} %get-tuple-element.364, bf16[3072,128]{1,0:T(8,128)(2,1)S(1)} %all_gather.18, bf16[4096,128]{1,0:T(8,128)(2,1)S(1)} %copy-done.60, s32[]{:T(128)S(6)} %select_n.66), kind=kOutput, calls=%fused_computation.69 | convolution fusion | flops 852492288 | bytes 45088772 | tf_op jit(solution)/shard_map/dot_general | solution.py:29
  614.2 9.2 fusion.138
  623.4 12.0 %add_convert_fusion.1 = bf16[3072,1024]{1,0:T(8,128)(2,1)} fusion(f32[3072,1024]{1,0:T(8,128)} %fusion.138, f32[3072,1024]{1,0:T(8,128)} %fusion.130, bf16[1024,128]{1,0:T(8,128)(2,1)S(1)} %copy-done.38, f32[3072,128]{1,0:T(8,128)S(1)} %fusion.94), kind=kOutput, calls=%fused_computation.68 | convolution fusion | flops 816316416 | bytes 33292288 | tf_op jit(solution)/shard_map/dot_general | solution.py:29
  635.5 9.9 fusion.136
  701.6 40.5 %all-reduce.4 = (f32[1024]{0:T(1024)}, f32[1024]{0:T(1024)}, f32[1024]{0:T(1024)}, f32[1024]{0:T(1024)}) all-reduce(f32[1024]{0:T(1024)S(1)} %get-tuple-element.285, f32[1024]{0:T(1024)S(1)} %get-tuple-element.288, f32[1024]{0:T(1024)S(1)} %get-tuple-element.280, ...), channel_id=1, replica_groups=mesh['dp'=8,'mp'=4] {'dp','mp'}, use_global_device_ids=true, to_apply=%region_21.22 | all-reduce | flops 4096 | bytes 32768 | tf_op jit(solution)/shard_map/psum | solution.py:333
  747.5 48.9 %reduce-scatter.6.cloned.1.call-done = f32[768,1024]{1,0:T(8,128)} async-done(((f32[3072,1024]{1,0:T(8,128)}), f32[768,1024]{1,0:T(8,128)}) %reduce-scatter.6.cloned.1.call-update) | async-done | bytes 3145744 | tf_op jit(solution)/shard_map/reduce_scatter | solution.py:275
  801.4 184.1 %all-reduce.8.cloned.1.call-done = (f32[1024,128]{1,0:T(8,128)}, f32[128,3072]{1,0:T(8,128)}, f32[1024,128]{1,0:T(8,128)}, f32[128,1024]{1,0:T(8,128)}, f32[1024...) async-done(((f32[1024,128]{1,0:T(8,128)}, f32[128,3072]{1,0:T(8,128)}, f32[1024,128]{1,0:T(8,128)}, f32[128,1024]{1,0:T(8,128)}, ...) | async-done | bytes 8388624 | tf_op jit(solution)/shard_map/psum | solution.py:333
  (434 shorter events, 451.7 us)
Async XLA Ops:
  7.2 448.8 %copy-start = (bf16[1024,1024]{1,0:T(8,128)(2,1)S(1)}, bf16[1024,1024]{1,0:T(8,128)(2,1)}, u32[]{:S(2)}) copy-start(bf16[1024,1024]{1,0:T(8,128)(2,1)} %param.35) | copy-start | bytes 6291460
  7.2 56.2 %all-gather.4.cloned.1.call-start = ((), (), s32[]{:S(2)}) async-start(), calls=%async_computation.5 | async-start | bytes 7864320 | tf_op jit(solution)/shard_map/all_gather | solution.py:250
  14.4 49.0 %copy-start.35 = (bf16[1024,128]{1,0:T(8,128)(2,1)S(1)}, bf16[1024,128]{1,0:T(8,128)(2,1)}, u32[]{:S(2)}) copy-start(bf16[1024,128]{1,0:T(8,128)(2,1)} %param.30) | copy-start | bytes 786436
  14.4 191.4 %all-gather.8.cloned.1.call-start = ((), (), s32[]{:S(2)}) async-start(), calls=%async_computation.10 | async-start | bytes 7864320 | tf_op jit(solution)/shard_map/all_gather | solution.py:293
  15.1 436.1 %all-gather.6.cloned.1.call-start = ((), (), s32[]{:S(2)}) async-start(), calls=%async_computation.6 | async-start | bytes 7864320 | tf_op jit(solution)/shard_map/all_gather | solution.py:251
  15.9 664.7 %reduce-scatter.8.cloned.1.call-start = ((), (), s32[]{:S(2)}) async-start(), calls=%async_computation.8 | async-start | bytes 1966080 | tf_op jit(solution)/shard_map/reduce_scatter | solution.py:276
  135.2 70.5 %copy-start.50 = (bf16[256,1024]{1,0:T(8,128)(2,1)S(1)}, bf16[256,1024]{1,0:T(8,128)(2,1)}, u32[]{:S(2)}) copy-start(bf16[256,1024]{1,0:T(8,128)(2,1)} %param.32) | copy-start | bytes 1572868
  451.2 232.2 %reduce-scatter.10.cloned.1.call-start = ((), (), s32[]{:S(2)}) async-start(), calls=%async_computation.9 | async-start | bytes 1966080 | tf_op jit(solution)/shard_map/reduce_scatter | solution.py:277
  456.0 39.1 %slice-start.10 = ((s8[6291456]{0:T(1024)(128)(4,1)}), s8[2097152]{0:T(1024)(128)(4,1)S(1)}, s32[]{:S(2)}) async-start(s8[6291456]{0:T(1024)(128)(4,1)} %bitcast.237), calls=%async_computation.24 | async-start | bytes 4194304
  462.8 32.3 %copy-start.16 = (f32[5,512,4,64]{1,3,2,0:T(8,128)S(1)}, f32[5,512,4,64]{1,3,2,0:T(8,128)}, u32[]{:S(2)}) copy-start(f32[5,512,4,64]{1,3,2,0:T(8,128)} %slice.97) | copy-start | bytes 7864324
  462.8 32.3 %slice-start.11 = ((s8[6291456]{0:T(1024)(128)(4,1)}), s8[4194304]{0:T(1024)(128)(4,1)S(1)}, s32[]{:S(2)}) async-start(s8[6291456]{0:T(1024)(128)(4,1)} %bitcast.237), calls=%async_computation.25 | async-start | bytes 8388608
  529.8 159.7 %reduce-scatter.14.cloned.1.call-start = ((), (), s32[]{:S(2)}) async-start(), calls=%async_computation.12 | async-start | bytes 7864320 | tf_op jit(solution)/shard_map/reduce_scatter | solution.py:323
  538.0 10.7 %copy-start.4 = (f32[3072,128]{1,0:T(8,128)S(1)}, f32[3072,128]{1,0:T(8,128)}, u32[]{:S(2)}) copy-start(f32[3072,128]{1,0:T(8,128)} %fusion.97) | copy-start | bytes 4718596
  560.9 133.0 %reduce-scatter.12.cloned.1.call-start = ((), (), s32[]{:S(2)}) async-start(), calls=%async_computation.11 | async-start | bytes 7864320 | tf_op jit(solution)/shard_map/reduce_scatter | solution.py:326
  572.6 13.6 %copy-start.48 = (bf16[3072,128]{1,0:T(8,128)(2,1)}, bf16[3072,128]{1,0:T(8,128)(2,1)S(1)}, u32[]{:S(2)}) copy-start(bf16[3072,128]{1,0:T(8,128)(2,1)S(1)} %all_gather.18) | copy-start | bytes 2359300
  603.0 11.2 %slice-start = ((s8[6291456]{0:T(1024)(128)(4,1)}), s8[4194304]{0:T(1024)(128)(4,1)S(1)}, s32[]{:S(2)}) async-start(s8[6291456]{0:T(1024)(128)(4,1)} %bitcast.215), calls=%async_computation.14 | async-start | bytes 8388608
  607.8 15.6 %copy-start.7 = (f32[3072,128]{1,0:T(8,128)}, f32[3072,128]{1,0:T(8,128)S(1)}, u32[]{:S(2)}) copy-start(f32[3072,128]{1,0:T(8,128)S(1)} %fusion.94) | copy-start | bytes 4718596
  635.4 10.0 copy-start.51
  635.4 161.0 %reduce-scatter.6.cloned.1.call-start = ((), (), s32[]{:S(2)}) async-start(), calls=%async_computation.7 | async-start | bytes 15728640 | tf_op jit(solution)/shard_map/reduce_scatter | solution.py:275
  651.9 333.6 %all-reduce.8.cloned.1.call-start = ((), (), s32[]{:S(2)}) async-start(), calls=%async_computation.13 | async-start | bytes 16777216 | tf_op jit(solution)/shard_map/psum | solution.py:333
  655.3 15.8 %slice-start.4 = ((s8[6291456]{0:T(1024)(128)(4,1)}), s8[4194304]{0:T(1024)(128)(4,1)S(1)}, s32[]{:S(2)}) async-start(s8[6291456]{0:T(1024)(128)(4,1)} %bitcast.228), calls=%async_computation.18 | async-start | bytes 8388608
  661.8 11.1 %slice-start.6 = ((s8[6291456]{0:T(1024)(128)(4,1)}), s8[4194304]{0:T(1024)(128)(4,1)S(1)}, s32[]{:S(2)}) async-start(s8[6291456]{0:T(1024)(128)(4,1)} %bitcast.230), calls=%async_computation.20 | async-start | bytes 8388608
  742.1 54.3 %copy-start.33 = (f32[768,128]{1,0:T(8,128)S(1)}, f32[768,128]{1,0:T(8,128)}, u32[]{:S(2)}) copy-start(f32[768,128]{1,0:T(8,128)} %reduce-scatter.10.cloned.1.call-done) | copy-start | bytes 1179652
  742.1 54.3 %copy-start.41 = (bf16[128,1024]{1,0:T(8,128)(2,1)S(1)}, bf16[128,1024]{1,0:T(8,128)(2,1)}, u32[]{:S(2)}) copy-start(bf16[128,1024]{1,0:T(8,128)(2,1)} %param.40) | copy-start | bytes 786436
  (74 other events, 358.2 us)
Sparse Core Ops, SparseCore 0:
  14.5 48.8 all-gather.3
  65.0 46.8 all-gather.7
  114.0 46.3 all-gather.5
  451.3 28.1 reduce-scatter.7
  529.9 28.1 reduce-scatter.9
  561.1 58.3 reduce-scatter.13
  635.5 58.3 reduce-scatter.11
  696.6 99.7 reduce-scatter.5
  804.0 181.4 all-reduce.7
where the time goes:
time: 1010 us; the launch traced here: 1000 us
  matrix products  382 us (38%)
  waiting for transfers between devices  272 us (27%)
  local copies, waits for them, and re-layouts  190 us (19%)
  other arithmetic  74.2 us (7%)
  blocking collectives  59.9 us (6%)
  between operations  15.1 us (1%)
    psum x1, waiting for transfers between devices, shards(): lax.psum((norm_grads[1], norm_grads[2], norm_grads[3], norm_grads[4], tri...  184 us
    dot_general x14, matrix products, dot_tail(): lax.dot_general(former, latter, (((1,), (1,)), ((), ())), preferred_eleme...  110 us
    dot_general x12, matrix products, dot_plain(): return jnp.dot(former, latter, preferred_element_type=jnp.float32)  85.7 us
    dynamic_update_slice x12, local copies, waits for them, and re-layouts, attend_forward(): lax.map(one_block, (query_blocks, key_windows(key_rows), key_windows(valu...  72.2 us
    reduce_scatter x1, waiting for transfers between devices, shards(): lax.psum_scatter(partial_out, 'mp', scatter_dimension=0, tiled=True)  48.9 us
    psum x1, blocking collectives, shards(): lax.psum((norm_grads[1], norm_grads[2], norm_grads[3], norm_grads[4], tri...  40.5 us
    dot_general x6, matrix products, one_block(): jnp.einsum('hqk,qhd->khd', weights_low, grad_blk, preferred_element_type=...  40.5 us
    all_gather x1, waiting for transfers between devices, shards(): lax.all_gather(normed_first.astype(jnp.bfloat16), 'mp', axis=0, tiled=True)  33.2 us
  transfers between devices with their start and end apart: 9, of which 4 were waited for; matrix products, arithmetic and copies ran while one was open for 61% of the time, Pallas kernels for 0%

commit v1 on v0

v1 whole, which is shorter than its diff:
```python
import functools
import math

import jax
import jax.numpy as jnp
import numpy as np
from jax import lax
from jax.experimental import pallas as pl
from jax.experimental.pallas import tpu as pltpu
from jax.sharding import PartitionSpec as P

HEAD_DIM = 64
ROT = 16
SHORT = 512
TOK_GRP = 3072
SLOTS = 6
EPS = 1e-05
LANES = 128
MESH = pl.DeviceIdType.MESH
BF16 = jnp.bfloat16
F32 = jnp.float32
VMEM_LIMIT = 56 * 1024 * 1024


def dot_nn(former, latter):
    return lax.dot_general(
        former, latter, (((1,), (0,)), ((), ())), preferred_element_type=F32
    )


def dot_nt(former, latter):
    return lax.dot_general(
        former, latter, (((1,), (1,)), ((), ())), preferred_element_type=F32
    )


def dot_tn(former, latter):
    return lax.dot_general(
        former, latter, (((0,), (0,)), ((), ())), preferred_element_type=F32
    )


def find_flags(group_lengths):
    seq_ends = jnp.cumsum(group_lengths, dtype=jnp.int32)
    starts = seq_ends - group_lengths
    block_starts = jnp.arange(SLOTS, dtype=jnp.int32) * SHORT
    begins = jnp.any(
        (starts[None, :] == block_starts[:, None]) & (group_lengths[None, :] > 0), axis=1
    )
    return jnp.where(begins, 0, 1).astype(jnp.int32)


def rotary_tables():
    half = ROT // 2
    frequency = np.exp(
        np.arange(half, dtype=np.float32) * np.float32(-2.0 * math.log(10000.0) / ROT)
    ).astype(np.float32)
    angles = np.arange(2 * SHORT, dtype=np.float32)[:, None] * frequency[None, :]
    cosine = np.ones((2 * SHORT, LANES), np.float32)
    minus = np.zeros((2 * SHORT, LANES), np.float32)
    plus = np.zeros((2 * SHORT, LANES), np.float32)
    for base in range(0, LANES, HEAD_DIM):
        cosine[:, base : base + half] = np.cos(angles)
        cosine[:, base + half : base + ROT] = np.cos(angles)
        minus[:, base : base + half] = -np.sin(angles)
        plus[:, base + half : base + ROT] = np.sin(angles)
    return jnp.asarray(cosine), jnp.asarray(minus), jnp.asarray(plus)


def gather_columns(width):
    old = np.arange(width).reshape(width // (3 * HEAD_DIM), 3, HEAD_DIM)
    order = old.transpose(1, 0, 2).reshape(-1)
    matrix = np.zeros((width, width), np.float32)
    matrix[order, np.arange(width)] = 1.0
    return jnp.asarray(matrix, BF16)


def rotate(pair, cosine, minus, plus):
    half = ROT // 2
    return (
        pair * cosine
        + pltpu.roll(pair, LANES - half, 1) * minus
        + pltpu.roll(pair, half, 1) * plus
    )


def unrotate(pair, cosine, minus, plus):
    half = ROT // 2
    return (
        pair * cosine
        - pltpu.roll(pair, LANES - half, 1) * minus
        - pltpu.roll(pair, half, 1) * plus
    )


def normalize(values, gain, shift):
    center = values - jnp.mean(values, axis=-1, keepdims=True)
    spread = jnp.mean(center * center, axis=-1, keepdims=True)
    return center * lax.rsqrt(spread + EPS) * gain + shift


def whole(shape):
    return pl.BlockSpec(
        shape, lambda *idx: (0,) * len(shape), pipeline_mode=pl.Buffered(1)
    )


def held(shape):
    return pl.BlockSpec(shape, lambda *idx: (0,) * len(shape))


def rows_of(tile, width):
    return pl.BlockSpec((tile, width), lambda i, *refs: (i, 0))


def shaped(shape, dtype):
    return jax.ShapeDtypeStruct(shape, dtype)


def params(semantics=1):
    return pltpu.CompilerParams(
        dimension_semantics=("arbitrary",) * semantics, vmem_limit_bytes=VMEM_LIMIT
    )


def unit_gather_kernel(unit, x_ref, d_ref, xg_ref, dg_ref, local_sem, send_sem, recv_sem):
    dp = lax.axis_index("dp")
    mp = lax.axis_index("mp")
    place = lax.rem(mp, unit)
    base = mp - place
    peers = [(dp, base + lax.rem(place + j, unit)) for j in range(1, unit)]
    barrier = pltpu.get_barrier_semaphore()
    for peer in peers:
        pl.semaphore_signal(barrier, inc=1, device_id=peer, device_id_type=MESH)
    pl.semaphore_wait(barrier, unit - 1)
    rows = x_ref.shape[0]
    span = pl.ds(pl.multiple_of(place * rows, rows), rows)
    copies = []
    for which, (src, dst) in enumerate(((x_ref, xg_ref), (d_ref, dg_ref))):
        for j, peer in enumerate(peers):
            copies.append(
                pltpu.make_async_remote_copy(
                    src_ref=src,
                    dst_ref=dst.at[span],
                    send_sem=send_sem.at[which, j],
                    recv_sem=recv_sem.at[which, j],
                    device_id=peer,
                    device_id_type=MESH,
                )
            )
        copies.append(pltpu.make_async_copy(src, dst.at[span], local_sem.at[which]))
    for copy in copies:
        copy.start()
    for copy in copies:
        copy.wait()


def unit_gather(unit, x, d):
    rows, width = x.shape
    anywhere = pl.BlockSpec(memory_space=pl.ANY)
    return pl.pallas_call(
        functools.partial(unit_gather_kernel, unit),
        out_shape=[shaped((rows * unit, width), x.dtype)] * 2,
        in_specs=[anywhere] * 2,
        out_specs=[anywhere] * 2,
        scratch_shapes=[
            pltpu.SemaphoreType.DMA((2,)),
            pltpu.SemaphoreType.DMA((2, unit - 1)),
            pltpu.SemaphoreType.DMA((2, unit - 1)),
        ],
        compiler_params=pltpu.CompilerParams(collective_id=1, has_side_effects=True),
        name="unit_gather",
    )(x, d)


def gelu_parts(hidden):
    cdf = 0.5 + 0.5 * lax.erf(hidden * math.sqrt(0.5))
    density = jnp.exp(-0.5 * hidden * hidden) * (1.0 / math.sqrt(2.0 * math.pi))
    return hidden * cdf, cdf + hidden * density


def feed_core(
    normed, low, dy, grad_low, up_ref, up_right_ref, down_ref, down_left_ref, act_ref, grad_ref, hidden_step
):
    hidden_width = up_ref.shape[1]
    for start in range(0, hidden_width, hidden_step):
        cols = pl.ds(start, hidden_step)
        hidden = dot_nn(normed, up_ref[:, cols]) + dot_nn(low, up_right_ref[:, cols])
        grad_act = dot_nt(dy, down_ref[cols, :]) + dot_nt(grad_low, down_left_ref[cols, :])
        activated, slope = gelu_parts(hidden)
        act_ref[:, cols] = activated.astype(BF16)
        grad_ref[:, cols] = (grad_act * slope).astype(BF16)


def feed_first_kernel(
    x_ref, dy_ref, gain_ref, shift_ref, up_ref, up_left_ref, up_right_ref, down_ref, down_left_ref, rights_ref,
    normed_ref, low_ref, grad_lows_ref, out_ref, grad_ref, low_act_ref, grad_low_ref, up_right_grad_ref,
    down_left_grad_ref, act_ref, gh_ref,
):
    normed = normalize(x_ref[...].astype(F32), gain_ref[...], shift_ref[...]).astype(BF16)
    normed_ref[...] = normed
    dy = dy_ref[...]
    low = dot_nn(normed, up_left_ref[...]).astype(BF16)
    low_ref[...] = low
    grad_lows = dot_nt(dy, rights_ref[...]).astype(BF16)
    grad_lows_ref[...] = grad_lows
    grad_low = grad_lows[:, LANES:]
    feed_core(normed, low, dy, grad_low, up_ref, up_right_ref, down_ref, down_left_ref, act_ref, gh_ref, 256)
    act = act_ref[...]
    gh = gh_ref[...]
    out_ref[...] = dot_nn(act, down_ref[...])
    grad_ref[...] = dot_nt(gh, up_ref[...])
    low_act_ref[...] = dot_nn(act, down_left_ref[...])
    grad_low_ref[...] = dot_nt(gh, up_right_ref[...])

    @pl.when(pl.program_id(0) == 0)
    def _():
        up_right_grad_ref[...] = jnp.zeros_like(up_right_grad_ref)
        down_left_grad_ref[...] = jnp.zeros_like(down_left_grad_ref)

    up_right_grad_ref[...] += dot_tn(low, gh)
    down_left_grad_ref[...] += dot_tn(grad_low, act)


def feed_first(x, dy, gain, shift, up, up_left, up_right, down, down_left, rights, tile):
    rows, width = x.shape
    hidden = up.shape[1]
    return pl.pallas_call(
        feed_first_kernel,
        grid=(rows // tile,),
        in_specs=[
            rows_of(tile, width),
            rows_of(tile, width),
            whole((1, width)),
            whole((1, width)),
            whole(up.shape),
            whole(up_left.shape),
            whole(up_right.shape),
            whole(down.shape),
            whole(down_left.shape),
            whole(rights.shape),
        ],
        out_specs=[
            rows_of(tile, width),
            rows_of(tile, LANES),
            rows_of(tile, 2 * LANES),
            rows_of(tile, width),
            rows_of(tile, width),
            rows_of(tile, LANES),
            rows_of(tile, LANES),
            held((LANES, hidden)),
            held((LANES, hidden)),
        ],
        out_shape=[
            shaped((rows, width), BF16),
            shaped((rows, LANES), BF16),
            shaped((rows, 2 * LANES), BF16),
            shaped((rows, width), F32),
            shaped((rows, width), F32),
            shaped((rows, LANES), F32),
            shaped((rows, LANES), F32),
            shaped((LANES, hidden), F32),
            shaped((LANES, hidden), F32),
        ],
        scratch_shapes=[pltpu.VMEM((tile, hidden), BF16), pltpu.VMEM((tile, hidden), BF16)],
        compiler_params=params(),
        cost_estimate=pl.CostEstimate(
            flops=10 * rows * width * hidden, bytes_accessed=30 * rows * width, transcendentals=2 * rows * hidden
        ),
        name="feed_first",
    )(x, dy, gain, shift, up, up_left, up_right, down, down_left, rights)


def feed_second_kernel(
    send_tiles, order_ref, normed_ref, low_ref, dy_ref, grad_lows_ref, out_in_ref, grad_in_ref, low_act_in_ref,
    grad_low_in_ref, up_ref, up_left_ref, up_right_ref, down_ref, down_left_ref, out_send_ref, out_keep_ref,
    grad_send_ref, grad_keep_ref, low_act_send_ref, low_act_keep_ref, up_right_grad_ref, down_left_grad_ref,
    up_left_grad_ref, act_ref, gh_ref,
):
    step = pl.program_id(0)
    normed = normed_ref[...]
    low = low_ref[...]
    dy = dy_ref[...]
    grad_low = grad_lows_ref[:, LANES:]
    feed_core(normed, low, dy, grad_low, up_ref, up_right_ref, down_ref, down_left_ref, act_ref, gh_ref, 256)
    act = act_ref[...]
    gh = gh_ref[...]
    grad_low_up = (grad_low_in_ref[...] + dot_nt(gh, up_right_ref[...])).astype(BF16)
    out = (out_in_ref[...] + dot_nn(act, down_ref[...])).astype(BF16)
    low_act = (low_act_in_ref[...] + dot_nn(act, down_left_ref[...])).astype(BF16)
    grad = (
        grad_in_ref[...] + dot_nt(gh, up_ref[...]) + dot_nt(grad_low_up, up_left_ref[...])
    ).astype(BF16)

    @pl.when(step < send_tiles)
    def _():
        out_send_ref[...] = out
        grad_send_ref[...] = grad
        low_act_send_ref[...] = low_act

    @pl.when(step >= send_tiles)
    def _():
        out_keep_ref[...] = out
        grad_keep_ref[...] = grad
        low_act_keep_ref[...] = low_act

    @pl.when(step == 0)
    def _():
        up_right_grad_ref[...] = jnp.zeros_like(up_right_grad_ref)
        down_left_grad_ref[...] = jnp.zeros_like(down_left_grad_ref)
        up_left_grad_ref[...] = jnp.zeros_like(up_left_grad_ref)

    up_right_grad_ref[...] += dot_tn(low, gh)
    down_left_grad_ref[...] += dot_tn(grad_low, act)
    up_left_grad_ref[...] += dot_tn(grad_low_up, normed)


def ordered(tile, width):
    return pl.BlockSpec((tile, width), lambda i, order: (order[i], 0))


def sent(tile, width, tiles):
    return pl.BlockSpec((tile, width), lambda i, order: (jnp.minimum(i, tiles - 1), 0))


def kept(tile, width, tiles):
    return pl.BlockSpec((tile, width), lambda i, order: (jnp.maximum(i - tiles, 0), 0))


def feed_second(order, normed, low, dy, grad_lows, out, grad, low_act, grad_low, up, up_left, up_right, down,
                down_left, own_rows, tile):
    rows, width = normed.shape
    hidden = up.shape[1]
    send_rows = rows - own_rows
    tiles = send_rows // tile
    return pl.pallas_call(
        functools.partial(feed_second_kernel, tiles),
        grid_spec=pltpu.PrefetchScalarGridSpec(
            num_scalar_prefetch=1,
            grid=(rows // tile,),
            in_specs=[
                ordered(tile, width),
                ordered(tile, LANES),
                ordered(tile, width),
                ordered(tile, 2 * LANES),
                ordered(tile, width),
                ordered(tile, width),
                ordered(tile, LANES),
                ordered(tile, LANES),
                whole(up.shape),
                whole(up_left.shape),
                whole(up_right.shape),
                whole(down.shape),
                whole(down_left.shape),
            ],
            out_specs=[
                sent(tile, width, tiles),
                kept(tile, width, tiles),
                sent(tile, width, tiles),
                kept(tile, width, tiles),
                sent(tile, LANES, tiles),
                kept(tile, LANES, tiles),
                held((LANES, hidden)),
                held((LANES, hidden)),
                held((LANES, width)),
            ],
            scratch_shapes=[pltpu.VMEM((tile, hidden), BF16), pltpu.VMEM((tile, hidden), BF16)],
        ),
        out_shape=[
            shaped((send_rows, width), BF16),
            shaped((own_rows, width), BF16),
            shaped((send_rows, width), BF16),
            shaped((own_rows, width), BF16),
            shaped((send_rows, LANES), BF16),
            shaped((own_rows, LANES), BF16),
            shaped((LANES, hidden), F32),
            shaped((LANES, hidden), F32),
            shaped((LANES, width), F32),
        ],
        compiler_params=params(),
        cost_estimate=pl.CostEstimate(
            flops=10 * rows * width * hidden, bytes_accessed=30 * rows * width, transcendentals=2 * rows * hidden
        ),
        name="feed_second",
    )(order, normed, low, dy, grad_lows, out, grad, low_act, grad_low, up, up_left, up_right, down, down_left)


def project_body(
    normed, low, dy_ref, grad_lows_ref, triple_ref, right_ref, output_ref, output_left_ref, cos_ref, minus_ref,
    plus_ref, q_ref, k_ref, v_ref, g_ref,
):
    tables = (cos_ref[...], minus_ref[...], plus_ref[...])
    head_width = output_ref.shape[0]
    mixed = dot_nn(normed, triple_ref[...]) + dot_nn(low, right_ref[...])
    for start in range(0, head_width, LANES):
        cols = slice(start, start + LANES)
        query = rotate(mixed[:, cols], *tables).astype(BF16)
        q_ref[:, cols] = query * HEAD_DIM**-0.5
        k_ref[:, cols] = rotate(
            mixed[:, head_width + start : head_width + start + LANES], *tables
        ).astype(BF16)
    v_ref[...] = mixed[:, 2 * head_width :].astype(BF16)
    g_ref[...] = (
        dot_nt(dy_ref[...], output_ref[...]) + dot_nt(grad_lows_ref[:, :LANES], output_left_ref[...])
    ).astype(BF16)


def project_first_kernel(
    cont_ref, x_ref, dy_ref, grad_lows_ref, gain_ref, shift_ref, triple_ref, left_ref, right_ref, output_ref,
    output_left_ref, cos_ref, minus_ref, plus_ref, normed_ref, low_ref, q_ref, k_ref, v_ref, g_ref,
):
    normed = normalize(x_ref[...].astype(F32), gain_ref[...], shift_ref[...]).astype(BF16)
    normed_ref[...] = normed
    low = dot_nn(normed, left_ref[...]).astype(BF16)
    low_ref[...] = low
    project_body(
        normed, low, dy_ref, grad_lows_ref, triple_ref, right_ref, output_ref, output_left_ref, cos_ref, minus_ref,
        plus_ref, q_ref, k_ref, v_ref, g_ref,
    )


def project_second_kernel(
    cont_ref, normed_ref, low_ref, dy_ref, grad_lows_ref, triple_ref, right_ref, output_ref, output_left_ref, cos_ref,
    minus_ref, plus_ref, q_ref, k_ref, v_ref, g_ref,
):
    project_body(
        normed_ref[...], low_ref[...], dy_ref, grad_lows_ref, triple_ref, right_ref, output_ref, output_left_ref,
        cos_ref, minus_ref, plus_ref, q_ref, k_ref, v_ref, g_ref,
    )


def project(first, conts, inputs, dy, grad_lows, norm, triple, left, right, output, output_left, tables, tile):
    rows, width = dy.shape
    head_width = output.shape[0]
    per_block = SHORT // tile

    def table_index(i, cont):
        return (cont[i // per_block] * per_block + lax.rem(i, per_block), 0)

    table = pl.BlockSpec((tile, LANES), table_index)
    row_specs = [rows_of(tile, value.shape[1]) for value in inputs]
    row_specs += [rows_of(tile, width), rows_of(tile, 2 * LANES)]
    fixed = list(norm) + [triple] + ([left] if first else []) + [right, output, output_left]
    new_specs = [rows_of(tile, width), rows_of(tile, LANES)] if first else []
    new_shapes = [shaped((rows, width), BF16), shaped((rows, LANES), BF16)] if first else []
    return pl.pallas_call(
        project_first_kernel if first else project_second_kernel,
        grid_spec=pltpu.PrefetchScalarGridSpec(
            num_scalar_prefetch=1,
            grid=(rows // tile,),
            in_specs=row_specs + [whole(value.shape) for value in fixed] + [table] * 3,
            out_specs=new_specs + [rows_of(tile, head_width)] * 4,
        ),
        out_shape=new_shapes + [shaped((rows, head_width), BF16)] * 4,
        compiler_params=params(),
        cost_estimate=pl.CostEstimate(
            flops=8 * rows * width * head_width, bytes_accessed=8 * rows * width, transcendentals=0
        ),
        name="project_first" if first else "project_second",
    )(conts, *inputs, dy, grad_lows, *fixed, *tables)


def attend_rows(with_prev, start, count, q_ref, k_ref, v_ref, g_ref, kp_ref, vp_ref, tables, att_ref, gq_ref,
                dk_ref, dv_ref, dkp_ref, dvp_ref):
    first_head = lax.broadcasted_iota(jnp.int32, (1, LANES), 1) < HEAD_DIM
    span = pl.ds(start, count)
    known = start + count
    zero = jnp.zeros((), BF16)

    def stack(pair):
        return jnp.concatenate([jnp.where(first_head, pair, zero), jnp.where(first_head, zero, pair)], axis=0)

    def unstack(both):
        return jnp.where(first_head, both[:count], both[count:])

    queries = stack(q_ref[span, :])
    grads = stack(g_ref[span, :])
    keys = k_ref[pl.ds(0, known), :]
    values = v_ref[pl.ds(0, known), :]
    scores = dot_nt(queries, keys)
    row = lax.broadcasted_iota(jnp.int32, (2 * count, known), 0)
    column = lax.broadcasted_iota(jnp.int32, (2 * count, known), 1)
    row = jnp.where(row >= count, row - count, row) + start
    scores = jnp.where(column <= row, scores, -1e30)
    peak = jnp.max(scores, axis=1, keepdims=True)
    if with_prev:
        prev_scores = dot_nt(queries, kp_ref[...])
        peak = jnp.maximum(peak, jnp.max(prev_scores, axis=1, keepdims=True))
        prev_exp = jnp.exp(prev_scores - peak)
    exp = jnp.exp(scores - peak)
    total = jnp.sum(exp, axis=1, keepdims=True)
    if with_prev:
        total = total + jnp.sum(prev_exp, axis=1, keepdims=True)
    scale = 1.0 / total
    weights = exp * scale
    weights_low = weights.astype(BF16)
    attended = dot_nn(weights_low, values)
    grad_weights = dot_nt(grads, values)
    inner = jnp.sum(weights * grad_weights, axis=1, keepdims=True)
    if with_prev:
        prev_weights = prev_exp * scale
        prev_low = prev_weights.astype(BF16)
        attended = attended + dot_nn(prev_low, vp_ref[...])
        prev_grad = dot_nt(grads, vp_ref[...])
        inner = inner + jnp.sum(prev_weights * prev_grad, axis=1, keepdims=True)
        prev_ds = (prev_weights * (prev_grad - inner)).astype(BF16)
    ds = (weights * (grad_weights - inner)).astype(BF16)
    grad_query = dot_nn(ds, keys)
    if with_prev:
        grad_query = grad_query + dot_nn(prev_ds, kp_ref[...])
        dkp_ref[...] += dot_tn(prev_ds, queries)
        dvp_ref[...] += dot_tn(prev_low, grads)
    dk_ref[pl.ds(0, known), :] += dot_tn(ds, queries)
    dv_ref[pl.ds(0, known), :] += dot_tn(weights_low, grads)
    att_ref[span, :] = unstack(attended).astype(BF16)
    grad_query = unstack(grad_query) * HEAD_DIM**-0.5
    gq_ref[span, :] = unrotate(grad_query, *[table[start : start + count] for table in tables]).astype(BF16)


def attend_kernel(
    blocks, count, cont_ref, q_ref, k_ref, v_ref, g_ref, k_before_ref, v_before_ref, k_halo_ref, v_halo_ref, cos_ref,
    minus_ref, plus_ref, att_ref, gq_ref, gk_ref, gv_ref, dk_halo_ref, dv_halo_ref, kp_ref, vp_ref, dk_ref, dv_ref,
    dkp_ref, dvp_ref,
):
    step = pl.program_id(1)
    block = blocks - 1 - step
    continued = cont_ref[block]
    offset = pl.multiple_of(continued * SHORT, SHORT)
    tables = tuple(ref[pl.ds(offset, SHORT), :] for ref in (cos_ref, minus_ref, plus_ref))

    @pl.when(step == 0)
    def _():
        dk_ref[...] = jnp.zeros_like(dk_ref)
        dv_ref[...] = jnp.zeros_like(dv_ref)

    @pl.when(step > 0)
    def _():
        dk_ref[...] = dkp_ref[...]
        dv_ref[...] = dvp_ref[...]

    dkp_ref[...] = jnp.zeros_like(dkp_ref)
    dvp_ref[...] = jnp.zeros_like(dvp_ref)
    args = (q_ref, k_ref, v_ref, g_ref, kp_ref, vp_ref, tables, att_ref, gq_ref, dk_ref, dv_ref, dkp_ref, dvp_ref)

    @pl.when(continued == 0)
    def _():
        for start in range(0, SHORT, count):
            attend_rows(False, start, count, *args)

    @pl.when(continued != 0)
    def _():
        @pl.when(block == 0)
        def _():
            kp_ref[...] = k_halo_ref[...]
            vp_ref[...] = v_halo_ref[...]

        @pl.when(block != 0)
        def _():
            kp_ref[...] = k_before_ref[...]
            vp_ref[...] = v_before_ref[...]

        for start in range(0, SHORT, count):
            attend_rows(True, start, count, *args)

    gk_ref[...] = unrotate(dk_ref[...], *tables).astype(BF16)
    gv_ref[...] = dv_ref[...].astype(BF16)

    @pl.when(block == 0)
    def _():
        base = tuple(ref[pl.ds(0, SHORT), :] for ref in (cos_ref, minus_ref, plus_ref))
        dk_halo_ref[...] = unrotate(dkp_ref[...], *base).astype(BF16)
        dv_halo_ref[...] = dvp_ref[...].astype(BF16)


def attend(conts, q, k, v, g, k_halo, v_halo, tables, count):
    rows, head_width = q.shape
    blocks = rows // SHORT
    here = pl.BlockSpec((SHORT, LANES), lambda p, i, cont: (blocks - 1 - i, p))
    before = pl.BlockSpec((SHORT, LANES), lambda p, i, cont: (jnp.maximum(blocks - 2 - i, 0), p))
    halo = pl.BlockSpec((SHORT, LANES), lambda p, i, cont: (0, p))
    return pl.pallas_call(
        functools.partial(attend_kernel, blocks, count),
        grid_spec=pltpu.PrefetchScalarGridSpec(
            num_scalar_prefetch=1,
            grid=(head_width // LANES, blocks),
            in_specs=[here] * 4 + [before] * 2 + [halo] * 2 + [whole(table.shape) for table in tables],
            out_specs=[here] * 4 + [halo] * 2,
            scratch_shapes=[pltpu.VMEM((SHORT, LANES), BF16)] * 2 + [pltpu.VMEM((SHORT, LANES), F32)] * 4,
        ),
        out_shape=[shaped((rows, head_width), BF16)] * 4 + [shaped((SHORT, head_width), BF16)] * 2,
        compiler_params=params(2),
        cost_estimate=pl.CostEstimate(
            flops=12 * rows * 3 * SHORT * head_width, bytes_accessed=16 * rows * head_width,
            transcendentals=rows * SHORT * head_width // HEAD_DIM,
        ),
        name="attend",
    )(conts, q, k, v, g, k, v, k_halo, v_halo, *tables)


def settle_kernel(
    send_tiles, halo_start, order_ref, normed_ref, low_ref, grad_lows_ref, out_in_ref,
    att0_ref, att1_ref, gq0_ref, gq1_ref, gk0_ref, gk1_ref, gv0_ref, gv1_ref, hk0_ref, hk1_ref, hv0_ref, hv1_ref,
    triple0_ref, triple1_ref, right0_ref, right1_ref, left_ref, output0_ref, output1_ref, output_left0_ref,
    output_left1_ref, out_ref, grad_send_ref, grad_keep_ref, low_att_send_ref, low_att_keep_ref, right_grad0_ref,
    right_grad1_ref, left_grad_ref, output_left_grad0_ref, output_left_grad1_ref,
):
    step = pl.program_id(0)
    here = (order_ref[step] >= halo_start).astype(F32)
    normed = normed_ref[...]
    low = low_ref[...]
    grad_low_out = grad_lows_ref[:, :LANES]
    att0, att1 = att0_ref[...], att1_ref[...]

    def mixed(gq, gk, gv, hk, hv):
        key = (gk[...].astype(F32) + here * hk[...].astype(F32)).astype(BF16)
        value = (gv[...].astype(F32) + here * hv[...].astype(F32)).astype(BF16)
        return jnp.concatenate([gq[...], key, value], axis=1)

    grad0 = mixed(gq0_ref, gk0_ref, gv0_ref, hk0_ref, hv0_ref)
    grad1 = mixed(gq1_ref, gk1_ref, gv1_ref, hk1_ref, hv1_ref)
    grad_low = (dot_nt(grad0, right0_ref[...]) + dot_nt(grad1, right1_ref[...])).astype(BF16)
    grad = (
        dot_nt(grad0, triple0_ref[...]) + dot_nt(grad1, triple1_ref[...]) + dot_nt(grad_low, left_ref[...])
    ).astype(BF16)
    out_ref[...] = out_in_ref[...] + dot_nn(att0, output0_ref[...]) + dot_nn(att1, output1_ref[...])
    low_att = (dot_nn(att0, output_left0_ref[...]) + dot_nn(att1, output_left1_ref[...])).astype(BF16)

    @pl.when(step < send_tiles)
    def _():
        grad_send_ref[...] = grad
        low_att_send_ref[...] = low_att

    @pl.when(step >= send_tiles)
    def _():
        grad_keep_ref[...] = grad
        low_att_keep_ref[...] = low_att

    sums = (right_grad0_ref, right_grad1_ref, left_grad_ref, output_left_grad0_ref, output_left_grad1_ref)

    @pl.when(step == 0)
    def _():
        for ref in sums:
            ref[...] = jnp.zeros_like(ref)

    right_grad0_ref[...] += dot_tn(low, grad0)
    right_grad1_ref[...] += dot_tn(low, grad1)
    left_grad_ref[...] += dot_tn(grad_low, normed)
    output_left_grad0_ref[...] += dot_tn(grad_low_out, att0)
    output_left_grad1_ref[...] += dot_tn(grad_low_out, att1)


def settle(order, normed, low, grad_lows, out, pairs, halos, weights, own_rows, tile):
    rows, width = normed.shape
    head_width = pairs[0].shape[1]
    send_rows = rows - own_rows
    tiles = send_rows // tile
    halo_start = (rows - SHORT) // tile
    halo = pl.BlockSpec((tile, head_width), lambda i, order: (jnp.maximum(order[i] - halo_start, 0), 0))
    return pl.pallas_call(
        functools.partial(settle_kernel, tiles, halo_start),
        grid_spec=pltpu.PrefetchScalarGridSpec(
            num_scalar_prefetch=1,
            grid=(rows // tile,),
            in_specs=[ordered(tile, width), ordered(tile, LANES), ordered(tile, 2 * LANES), ordered(tile, width)]
            + [ordered(tile, head_width)] * 8
            + [halo] * 4
            + [whole(value.shape) for value in weights],
            out_specs=[
                ordered(tile, width),
                sent(tile, width, tiles),
                kept(tile, width, tiles),
                sent(tile, LANES, tiles),
                kept(tile, LANES, tiles),
                held((LANES, 3 * head_width)),
                held((LANES, 3 * head_width)),
                held((LANES, width)),
                held((LANES, head_width)),
                held((LANES, head_width)),
            ],
        ),
        out_shape=[
            shaped((rows, width), F32),
            shaped((send_rows, width), BF16),
            shaped((own_rows, width), BF16),
            shaped((send_rows, LANES), BF16),
            shaped((own_rows, LANES), BF16),
            shaped((LANES, 3 * head_width), F32),
            shaped((LANES, 3 * head_width), F32),
            shaped((LANES, width), F32),
            shaped((LANES, head_width), F32),
            shaped((LANES, head_width), F32),
        ],
        compiler_params=params(),
        cost_estimate=pl.CostEstimate(
            flops=20 * rows * width * head_width, bytes_accessed=16 * rows * width, transcendentals=0
        ),
        name="settle",
    )(order, normed, low, grad_lows, out, *pairs, *halos, *weights)


def finish_kernel(
    peers, x_ref, dy_ref, gain1_ref, gain2_ref, output_right_ref, shrink_right_ref, out_ref, first_ref, second_ref,
    low_att_ref, low_act_ref, *refs,
):
    others = refs[: 5 * peers]
    y_ref, dx_ref, norms_ref, output_right_grad_ref, shrink_right_grad_ref = refs[5 * peers :]

    def total(own, which):
        value = own[...].astype(F32)
        for j in range(peers):
            value = value + others[5 * j + which][...].astype(F32)
        return value

    out = total(out_ref, 0)
    first = total(first_ref, 1)
    second = total(second_ref, 2)
    low_att = total(low_att_ref, 3).astype(BF16)
    low_act = total(low_act_ref, 4).astype(BF16)
    x = x_ref[...].astype(F32)
    dy = dy_ref[...]
    y_ref[...] = (
        x + out + dot_nn(low_att, output_right_ref[...]) + dot_nn(low_act, shrink_right_ref[...])
    ).astype(BF16)
    center = x - jnp.mean(x, axis=-1, keepdims=True)
    spread = jnp.mean(center * center, axis=-1, keepdims=True)
    inverse = lax.rsqrt(spread + EPS)
    unit = center * inverse
    scaled = first * gain1_ref[...] + second * gain2_ref[...]
    mean = jnp.mean(scaled, axis=-1, keepdims=True)
    inner = jnp.mean(scaled * unit, axis=-1, keepdims=True)
    dx_ref[...] = dy.astype(F32) + (scaled - mean - unit * inner) * inverse

    @pl.when(pl.program_id(0) == 0)
    def _():
        norms_ref[...] = jnp.zeros_like(norms_ref)
        output_right_grad_ref[...] = jnp.zeros_like(output_right_grad_ref)
        shrink_right_grad_ref[...] = jnp.zeros_like(shrink_right_grad_ref)

    norms_ref[0:1, :] += jnp.sum(first * unit, axis=0, keepdims=True)
    norms_ref[1:2, :] += jnp.sum(first, axis=0, keepdims=True)
    norms_ref[2:3, :] += jnp.sum(second * unit, axis=0, keepdims=True)
    norms_ref[3:4, :] += jnp.sum(second, axis=0, keepdims=True)
    output_right_grad_ref[...] += dot_tn(low_att, dy)
    shrink_right_grad_ref[...] += dot_tn(low_act, dy)


def finish(x, dy, gain1, gain2, output_right, shrink_right, own, others, tile):
    rows, width = x.shape
    peers = len(others)
    widths = (width, width, width, LANES, LANES)
    return pl.pallas_call(
        functools.partial(finish_kernel, peers),
        grid=(rows // tile,),
        in_specs=[rows_of(tile, width)] * 2
        + [whole((1, width))] * 2
        + [whole(output_right.shape)] * 2
        + [rows_of(tile, size) for size in widths] * (1 + peers),
        out_specs=[rows_of(tile, width)] * 2 + [held((8, width)), held((LANES, width)), held((LANES, width))],
        out_shape=[
            shaped((rows, width), BF16),
            shaped((rows, width), F32),
            shaped((8, width), F32),
            shaped((LANES, width), F32),
            shaped((LANES, width), F32),
        ],
        compiler_params=params(),
        cost_estimate=pl.CostEstimate(
            flops=60 * rows * width, bytes_accessed=20 * rows * width, transcendentals=0
        ),
        name="finish",
    )(x, dy, gain1, gain2, output_right, shrink_right, *own, *[value for other in others for value in other])


def shards(
    ranks,
    block_input,
    sequence_lengths,
    first_gain,
    first_shift,
    second_gain,
    second_shift,
    triple_weight,
    triple_left,
    triple_right,
    output_weight,
    output_left,
    output_right,
    expand_weight,
    expand_left,
    expand_right,
    shrink_weight,
    shrink_left,
    shrink_right,
    cotangent,
):
    unit = ranks // 2
    own_rows, width = block_input.shape
    rows = own_rows * unit
    blocks = rows // SHORT
    tile = math.gcd(own_rows, 256)
    triple_width = triple_weight.shape[1]
    head_width = output_weight.shape[0]
    hidden = expand_weight.shape[1]
    mp = lax.axis_index("mp")
    half = mp // unit
    place = lax.rem(mp, unit)
    far = lax.rem(mp + unit, ranks)
    swap = [(m, (m + unit) % ranks) for m in range(ranks)]
    onward = [(m, m + unit) for m in range(unit)]
    back = [(m + unit, m) for m in range(unit)]

    tables = rotary_tables()
    perm = gather_columns(triple_width)
    continues = find_flags(sequence_lengths[0])
    conts = lax.dynamic_slice_in_dim(continues, half * blocks, blocks, 0)
    per_device = own_rows // tile
    order = jnp.concatenate(
        [
            lax.rem(place + j, unit) * per_device + jnp.arange(per_device, dtype=jnp.int32)
            for j in list(range(1, unit)) + [0]
        ]
    ).astype(jnp.int32)

    def cols(matrix, size, shard):
        return lax.dynamic_slice_in_dim(matrix, shard * size, size, 1)

    def tall(matrix, size, shard):
        return lax.dynamic_slice_in_dim(matrix, shard * size, size, 0)

    def arranged(matrix):
        return jnp.dot(matrix, perm, preferred_element_type=F32).astype(BF16)

    triple_own = arranged(triple_weight)
    triple_far = lax.ppermute(triple_own, "mp", swap)
    output_far = lax.ppermute(output_weight, "mp", swap)
    expand_late, shrink_late, triple_far, output_far = lax.optimization_barrier(
        (expand_weight, shrink_weight, triple_far, output_far)
    )
    expand_far = lax.ppermute(expand_late, "mp", swap)
    shrink_far = lax.ppermute(shrink_late, "mp", swap)

    gain1, shift1 = first_gain[None, :], first_shift[None, :]
    gain2, shift2 = second_gain[None, :], second_shift[None, :]
    rights = jnp.concatenate([output_right, shrink_right], axis=0)

    x, dy = unit_gather(unit, block_input, cotangent)

    (normed2, low2, grad_lows, out, grad2, low_act, grad_low2, expand_right_own, shrink_left_own) = feed_first(
        x, dy, gain2, shift2, expand_weight, expand_left, cols(expand_right, hidden, mp), shrink_weight,
        tall(shrink_left, hidden, mp), rights, tile,
    )

    right_own = arranged(cols(triple_right, triple_width, mp))
    right_far = arranged(cols(triple_right, triple_width, far))
    output_left_own = tall(output_left, head_width, mp)
    output_left_far = tall(output_left, head_width, far)
    normed1, low1, q_own, k_own, v_own, g_own = project(
        True, conts, (x,), dy, grad_lows, (gain1, shift1), triple_own, triple_left, right_own, output_weight,
        output_left_own, tables, tile,
    )
    last = slice(rows - SHORT, rows)
    halo_far = lax.ppermute(jnp.concatenate([k_own[last], v_own[last]], axis=0), "mp", onward)
    q_far, k_far, v_far, g_far = project(
        False, conts, (normed1, low1), dy, grad_lows, (), triple_far, None, right_far, output_far, output_left_far,
        tables, tile,
    )
    halo_own = lax.ppermute(jnp.concatenate([k_far[last], v_far[last]], axis=0), "mp", onward)
    count = 256
    att_far, gq_far, gk_far, gv_far, hk, hv = attend(
        conts, q_far, k_far, v_far, g_far, halo_far[:SHORT], halo_far[SHORT:], tables, count
    )
    back_own = lax.ppermute(jnp.concatenate([hk, hv], axis=0), "mp", back)
    att_own, gq_own, gk_own, gv_own, hk, hv = attend(
        conts, q_own, k_own, v_own, g_own, halo_own[:SHORT], halo_own[SHORT:], tables, count
    )
    back_far = lax.ppermute(jnp.concatenate([hk, hv], axis=0), "mp", back)
    (out, grad1_send, grad1_keep, low_att_send, low_att_keep, triple_right_own, triple_right_far, triple_left_sum,
     output_left_sum_own, output_left_sum_far) = settle(
        order, normed1, low1, grad_lows, out,
        (att_own, att_far, gq_own, gq_far, gk_own, gk_far, gv_own, gv_far),
        (back_own[:SHORT], back_far[:SHORT], back_own[SHORT:], back_far[SHORT:]),
        (triple_own, triple_far, right_own, right_far, triple_left, output_weight, output_far, output_left_own,
         output_left_far),
        own_rows, tile,
    )

    (out_send, out_keep, grad2_send, grad2_keep, low_act_send, low_act_keep, expand_right_far, shrink_left_far,
     expand_left_sum) = feed_second(
        order, normed2, low2, dy, grad_lows, out, grad2, low_act, grad_low2, expand_far, expand_left,
        cols(expand_right, hidden, far), shrink_far, tall(shrink_left, hidden, far), own_rows, tile,
    )

    def pass_on(sent_rows):
        got = []
        for j in range(1, unit):
            ring = [(m, m - m % unit + (m % unit + j) % unit) for m in range(ranks)]
            got.append(lax.ppermute(sent_rows[(j - 1) * own_rows : j * own_rows], "mp", ring))
        return got

    sends = (out_send, grad1_send, grad2_send, low_att_send, low_act_send)
    arrived = list(zip(*[pass_on(value) for value in sends]))
    block_output, input_gradient, norms, output_right_sum, shrink_right_sum = finish(
        block_input, cotangent, gain1, gain2, output_right, shrink_right,
        (out_keep, grad1_keep, grad2_keep, low_att_keep, low_act_keep), arrived, tile,
    )

    def place(total, own, other, size):
        wide = jnp.zeros((LANES, total), BF16)
        wide = lax.dynamic_update_slice_in_dim(wide, own.astype(BF16), mp * size, 1)
        return lax.dynamic_update_slice_in_dim(wide, other.astype(BF16), far * size, 1)

    sums = lax.psum(
        (
            norms,
            triple_left_sum.astype(BF16),
            place(triple_right.shape[1], triple_right_own, triple_right_far, triple_width),
            place(output_left.shape[0], output_left_sum_own, output_left_sum_far, head_width),
            output_right_sum.astype(BF16),
            expand_left_sum.astype(BF16),
            place(expand_right.shape[1], expand_right_own, expand_right_far, hidden),
            place(shrink_left.shape[0], shrink_left_own, shrink_left_far, hidden),
            shrink_right_sum.astype(BF16),
        ),
        ("dp", "mp"),
    )
    norms = sums[0]
    sums = [value.astype(F32) for value in sums[1:]]
    triple_right_sum = (
        sums[1].reshape(LANES, ranks, 3, head_width // HEAD_DIM, HEAD_DIM).transpose(0, 1, 3, 2, 4)
    ).reshape(triple_right.shape)
    return (
        block_output,
        input_gradient,
        norms[0],
        norms[1],
        norms[2],
        norms[3],
        sums[0].T,
        triple_right_sum,
        sums[2].T,
        sums[3],
        sums[4].T,
        sums[5],
        sums[6].T,
        sums[7],
    )


def solution(mesh):
    placed = (
        P(("dp", "mp"), None),
        P("dp", None),
        P(),
        P(),
        P(),
        P(),
        P(None, "mp"),
        P(),
        P(),
        P("mp", None),
        P(),
        P(),
        P(None, "mp"),
        P(),
        P(),
        P("mp", None),
        P(),
        P(),
        P(("dp", "mp"), None),
    )
    return jax.shard_map(
        functools.partial(shards, mesh.shape["mp"]),
        mesh=mesh,
        in_specs=placed,
        out_specs=(P(("dp", "mp"), None), P(("dp", "mp"), None)) + (P(),) * 12,
        check_vma=False,
    )
```

time: 1010 us -> 584 us (0.58)
  matrix products: 382 us -> 5.85 us
  Pallas kernels: 0 us -> 249 us
  local copies, waits for them, and re-layouts: 190 us -> 24.1 us
  waiting for transfers between devices: 272 us -> 213 us
  other arithmetic: 74.2 us -> 15.7 us
  blocking collectives: 59.9 us -> 42.2 us
  starting transfers between devices: 0.37 us -> 16.7 us
    dot_general x78 -> x3, matrix products: 382 us -> 5.85 us  [arranged(): return jnp.dot(matrix, perm, preferred_element_type=F32).astype(BF16)]
    pallas_call x0 -> x9, Pallas kernels: none -> 249 us  [the longest x1 97.4 us: unit_gather(): pl.pallas_call(functools.partial(unit_gather_kernel, unit), out_shape=[sh...]
    ppermute x0 -> x13, waiting for transfers between devices: none -> 109 us  [the longest x1 88.3 us: shards(): back_far = lax.ppermute(jnp.concatenate([hk, hv], axis=0), 'mp', back)]
    psum x1, waiting for transfers between devices: 184 us -> 104 us  [shards(): lax.psum((norms, triple_left_sum.astype(BF16), place(triple_right.shape[1...]
    dynamic_update_slice x12 -> x8, local copies, waits for them, and re-layouts: 72.2 us -> 0.26 us  [the longest x4 0.14 us: place(): wide = lax.dynamic_update_slice_in_dim(wide, own.astype(BF16), mp * size, 1)]
    reduce_scatter x5 -> x0, waiting for transfers between devices: 53.4 us -> none  [the longest x1 48.9 us: shards(): lax.psum_scatter(partial_out, 'mp', scatter_dimension=0, tiled=True)]
    all_gather x3 -> x0, waiting for transfers between devices: 33.2 us -> none  [the longest x1 33.2 us: shards(): lax.all_gather(normed_first.astype(jnp.bfloat16), 'mp', axis=0, tiled=True)]
    reduce_sum x10 -> x0, other arithmetic: 25.3 us -> none  [the longest x6 14 us: one_block(): row_total = jnp.sum(exp_scores, axis=-1, keepdims=True)]
  transfers between devices with their start and end apart: 9 -> 14, of which waited for: 4 -> 4; matrix products, arithmetic and copies ran while one was open for 61% -> 4% of each run, Pallas kernels for 0% -> 39%
where the time goes in v1:
time: 584 us; the launch traced here: 581 us
  Pallas kernels  249 us (43%)
  waiting for transfers between devices  213 us (36%)
  blocking collectives  42.2 us (7%)
  local copies, waits for them, and re-layouts  24.1 us (4%)
  starting transfers between devices  16.7 us (3%)
  other arithmetic  15.7 us (3%)
  between operations  14.7 us (3%)
  matrix products  5.85 us (1%)
    psum x1, waiting for transfers between devices, shards(): lax.psum((norms, triple_left_sum.astype(BF16), place(triple_right.shape[1...  104 us
    pallas_call x1, Pallas kernels, unit_gather(): pl.pallas_call(functools.partial(unit_gather_kernel, unit), out_shape=[sh...  97.4 us
    ppermute x1, waiting for transfers between devices, shards(): back_far = lax.ppermute(jnp.concatenate([hk, hv], axis=0), 'mp', back)  88.3 us
    psum x1, blocking collectives, shards(): lax.psum((norms, triple_left_sum.astype(BF16), place(triple_right.shape[1...  42.2 us
    pallas_call x2, Pallas kernels, attend(): pl.pallas_call(functools.partial(attend_kernel, blocks, count), grid_spec...  38.1 us
    pallas_call x1, Pallas kernels, feed_second(): pl.pallas_call(functools.partial(feed_second_kernel, tiles), grid_spec=pl...  29.5 us
    pallas_call x1, Pallas kernels, feed_first(): pl.pallas_call(feed_first_kernel, grid=(rows // tile,), in_specs=[rows_of...  29.4 us
    pallas_call x2, Pallas kernels, project(): pl.pallas_call(project_first_kernel if first else project_second_kernel,...  23.2 us
  transfers between devices with their start and end apart: 14, of which 4 were waited for; matrix products, arithmetic and copies ran while one was open for 4% of the time, Pallas kernels for 39%

profile of v1, /device:TPU:1, one launch (start us, length us, event | category | flops | bytes accessed | tf_op | source)
XLA Modules:
  0.0 581.2 jit_solution(11260706816067905764)
XLA Ops:
  8.6 3.8 fusion.triple_ref.triple0_ref
  12.4 2.1 collective-permute-start
  15.5 1.9 constant_dynamic-slice_fusion.1
  17.4 97.4 %unit_gather.1 = (bf16[1536,1024]{1,0:T(8,128)(2,1)}, bf16[1536,1024]{1,0:T(8,128)(2,1)}) custom-call(bf16[768,1024]{1,0:T(8,128)(2,1)} %x_ref.3, bf16[768,1024]{1,0:T(8,128)(2,1)} %dy_ref.1), custom_call_target="tpu_custom_call" | custom-call | tf_op jit(solution)/shard_map/unit_gather/pallas_call | solution.py:161
  115.9 29.4 %feed_first.1 = (bf16[1536,1024]{1,0:T(8,128)(2,1)}, bf16[1536,128]{1,0:T(8,128)(2,1)}, bf16[1536,256]{1,0:T(8,128)(2,1)}, f32[1536,1024]{1,0:T(8,128)}, f32[153...) custom-call(bf16[1536,1024]{1,0:T(8,128)(2,1)} %get-tuple-element.75, ...), custom_call_target="tpu_custom_call" | custom-call | flops 16106127360 | bytes 47185920 | tf_op jit(solution)/shard_map/feed_first/pallas_call | solution.py:228
  147.6 12.8 %project_first.1 = (bf16[1536,1024]{1,0:T(8,128)(2,1)}, bf16[1536,128]{1,0:T(8,128)(2,1)}, bf16[1536,256]{1,0:T(8,128)(2,1)}, bf16[1536,256]{1,0:T(8,128)(2,1)},...) custom-call(s32[3]{0:T(128)} %dynamic_slice.29.cont_ref, bf16[1536,1024]{1,0:T(8,128)(2,1)} %get-tuple-element.75.x_ref, ...), custom_call_target="tpu_custom_call" | custom-call | flops 3221225472 | bytes 12582912 | tf_op jit(solution)/shard_map/project_first/pallas_call | solution.py:446
  162.4 1.7 collective-permute-start.3
  165.3 10.2 %collective-permute-done.3 = bf16[1024,256]{1,0:T(8,128)(2,1)S(1)} collective-permute-done((bf16[1024,256]{1,0:T(8,128)(2,1)S(1)}, bf16[1024,256]{1,0:T(8,128)(2,1)S(1)}, u32[]{:S(2)}, u32[]{:S(2)}) %collective-permute-start.3) | collective-permute-done | bytes 524320 | tf_op jit(solution)/shard_map/ppermute | solution.py:862
  176.3 10.5 %collective-permute-done.1.output_ref.output1_ref = bf16[256,1024]{1,0:T(8,128)(2,1)} collective-permute-done((bf16[256,1024]{1,0:T(8,128)(2,1)}, bf16[256,1024]{1,0:T(8,128)(2,1)}, u32[]{:S(2)}, u32[]{:S(2)}) %collective-permute-start.1) | collective-permute-done | bytes 524320 | tf_op jit(solution)/shard_map/ppermute | solution.py:835
  186.8 10.3 %project_second.1 = (bf16[1536,256]{1,0:T(8,128)(2,1)}, bf16[1536,256]{1,0:T(8,128)(2,1)}, bf16[1536,256]{1,0:T(8,128)(2,1)}, bf16[1536,256]{1,0:T(8,128)(2,1)}) custom-call(s32[3]{0:T(128)} %dynamic_slice.29.cont_ref, bf16[1536,1024]{1,0:T(8,128)(2,1)} %get-tuple-element.80.normed_ref, bf16[1536,128]{1,0:T(8,128)(2,1)} %get-tuple-element.81.low_ref, ...), custom_call_target="tpu_custom_call" | custom-call | flops 3221225472 | bytes 12582912 | tf_op jit(solution)/shard_map/project_second/pallas_call | solution.py:446
  199.1 4.3 collective-permute-start.2
  203.5 19.0 %attend.3 = (bf16[1536,256]{1,0:T(8,128)(2,1)}, bf16[1536,256]{1,0:T(8,128)(2,1)}, bf16[1536,256]{1,0:T(8,128)(2,1)}, bf16[1536,256]{1,0:T(8,128)(2,1)}, bf16[51...) custom-call(s32[3]{0:T(128)} %dynamic_slice.29.cont_ref, bf16[1536,256]{1,0:T(8,128)(2,1)} %get-tuple-element.92.q_ref, ...), custom_call_target="tpu_custom_call" | custom-call | flops 7247757312 | bytes 6291456 | tf_op jit(solution)/shard_map/attend/pallas_call | solution.py:581
  225.1 2.9 collective-permute-start.6
  228.9 19.0 %attend.2 = (bf16[1536,256]{1,0:T(8,128)(2,1)}, bf16[1536,256]{1,0:T(8,128)(2,1)}, bf16[1536,256]{1,0:T(8,128)(2,1)}, bf16[1536,256]{1,0:T(8,128)(2,1)}, bf16[51...) custom-call(s32[3]{0:T(128)} %dynamic_slice.29.cont_ref, bf16[1536,256]{1,0:T(8,128)(2,1)} %get-tuple-element.83.q_ref, ...), custom_call_target="tpu_custom_call" | custom-call | flops 7247757312 | bytes 6291456 | tf_op jit(solution)/shard_map/attend/pallas_call | solution.py:581
  252.0 88.3 %collective-permute-done.5 = bf16[1024,256]{1,0:T(8,128)(2,1)S(1)} collective-permute-done((bf16[1024,256]{1,0:T(8,128)(2,1)S(1)}, bf16[1024,256]{1,0:T(8,128)(2,1)S(1)}, u32[]{:S(2)}, u32[]{:S(2)}) %collective-permute-start.5) | collective-permute-done | bytes 524320 | tf_op jit(solution)/shard_map/ppermute | solution.py:876
  341.1 21.1 %settle.1 = (f32[1536,1024]{1,0:T(8,128)}, bf16[768,1024]{1,0:T(8,128)(2,1)}, bf16[768,1024]{1,0:T(8,128)(2,1)}, bf16[768,128]{1,0:T(8,128)(2,1)}, bf16[768,128]...) custom-call(s32[6]{0:T(128)} %pad_add_fusion.order_ref, ...), custom_call_target="tpu_custom_call" | custom-call | flops 8053063680 | bytes 25165824 | tf_op jit(solution)/shard_map/settle/pallas_call | solution.py:659
  363.6 29.5 %feed_second.1 = (bf16[768,1024]{1,0:T(8,128)(2,1)}, bf16[768,1024]{1,0:T(8,128)(2,1)}, bf16[768,1024]{1,0:T(8,128)(2,1)}, bf16[768,1024]{1,0:T(8,128)(2,1)}, bf...) custom-call(s32[6]{0:T(128)} %pad_add_fusion.order_ref, ...), custom_call_target="tpu_custom_call" | custom-call | flops 16106127360 | bytes 47185920 | tf_op jit(solution)/shard_map/feed_second/pallas_call | solution.py:336
  400.2 2.2 convert_bitcast_fusion
  403.1 10.3 %finish.1 = (bf16[768,1024]{1,0:T(8,128)(2,1)}, f32[768,1024]{1,0:T(8,128)}, f32[8,1024]{1,0:T(8,128)}, f32[128,1024]{1,0:T(8,128)}, f32[128,1024]{1,0:T(8,128)}) custom-call(bf16[768,1024]{1,0:T(8,128)(2,1)} %x_ref.3, bf16[768,1024]{1,0:T(8,128)(2,1)} %dy_ref.1, f32[1,1024]{1,0:T(1,128)} %bitcast.33, f32[1,1024]{1,0:T(1,128)} %bitcast.35, ...), custom_call_target="tpu_custom_call" | custom-call | flops 47185920 | bytes 15728640 | tf_op jit(solution)/shard_map/finish/pallas_call | solution.py:751
  413.4 1.8 convert_element_type.67
  415.2 1.8 convert_element_type.75
  417.7 42.2 %psum.63 = f32[8,1024]{1,0:T(8,128)S(1)} all-reduce(f32[8,1024]{1,0:T(8,128)S(1)} %copy-done.28), channel_id=1, replica_groups=mesh['dp'=8,'mp'=4] {'dp','mp'}, use_global_device_ids=true, to_apply=%region_2.3 | all-reduce | flops 8192 | bytes 65536 | tf_op jit(solution)/shard_map/psum | solution.py:912
  460.5 103.9 %all-reduce.3.cloned.1.call-done = (bf16[1024,128]{0,1:T(8,128)(2,1)}, bf16[128,3072]{0,1:T(8,128)(2,1)}, bf16[1024,128]{0,1:T(8,128)(2,1)}, bf16[128,4096]{0,1:...) async-done(((bf16[1024,128]{0,1:T(8,128)(2,1)}, bf16[128,3072]{0,1:T(8,128)(2,1)}, ...) | async-done | bytes 4194320 | tf_op jit(solution)/shard_map/psum | solution.py:912
  564.4 2.7 copy.74
  (147 shorter events, 37.5 us)
Async XLA Ops:
  7.2 7.3 %copy-start.30 = (s32[1,6]{1,0:T(1,128)S(1)}, s32[1,6]{1,0:T(1,128)}, u32[]{:S(2)}) copy-start(s32[1,6]{1,0:T(1,128)} %param.24) | copy-start | bytes 76
  7.2 7.5 %copy-start.21 = (bf16[4096,128]{1,0:T(8,128)(2,1)S(1)}, bf16[4096,128]{1,0:T(8,128)(2,1)}, u32[]{:S(2)}) copy-start(bf16[4096,128]{1,0:T(8,128)(2,1)} %param.39) | copy-start | bytes 3145732
  7.2 557.2 %all-reduce.3.cloned.1.call-start = ((), (), s32[]{:S(2)}) async-start(), calls=%async_computation | async-start | bytes 8388608 | tf_op jit(solution)/shard_map/psum | solution.py:912
  12.4 174.4 %collective-permute-start = (bf16[1024,768]{1,0:T(8,128)(2,1)}, bf16[1024,768]{1,0:T(8,128)(2,1)}, u32[]{:S(2)}, u32[]{:S(2)}) collective-permute-start(bf16[1024,768]{1,0:T(8,128)(2,1)} %fusion.triple_ref.triple0_ref), channel_id=1, source_target_pairs={{0,2},{1,3},{2,0},{3,1},{4,6},{5,7},{6,4},{7,5},{8,10},{9,11},{10,... | collective-permute-start | bytes 4718600 | tf_op jit(solution)/shard_map/ppermute | solution.py:834
  17.4 97.5 %copy-start.7 = (bf16[128,1024]{1,0:T(8,128)(2,1)S(1)}, bf16[128,1024]{1,0:T(8,128)(2,1)}, u32[]{:S(2)}) copy-start(bf16[128,1024]{1,0:T(8,128)(2,1)} %output_right_ref.1) | copy-start | bytes 786436
  17.4 97.5 %copy-start.8 = (bf16[128,1024]{1,0:T(8,128)(2,1)S(1)}, bf16[128,1024]{1,0:T(8,128)(2,1)}, u32[]{:S(2)}) copy-start(bf16[128,1024]{1,0:T(8,128)(2,1)} %shrink_right_ref.1) | copy-start | bytes 786436
  115.8 30.1 %copy-start.27 = (bf16[1024,128]{1,0:T(8,128)(2,1)S(1)}, bf16[1024,128]{1,0:T(8,128)(2,1)}, u32[]{:S(2)}) copy-start(bf16[1024,128]{1,0:T(8,128)(2,1)} %param.33) | copy-start | bytes 786436
  115.9 30.8 %copy-start.2 = (bf16[768,768]{1,0:T(8,128)(2,1)S(1)}, bf16[768,768]{1,0:T(8,128)(2,1)}, u32[]{:S(2)}) copy-start(bf16[768,768]{1,0:T(8,128)(2,1)} %constant.65.clone) | copy-start | bytes 3538948
  115.9 30.7 %copy-start.22 = (bf16[128,3072]{1,0:T(8,128)(2,1)S(1)}, bf16[128,3072]{1,0:T(8,128)(2,1)}, u32[]{:S(2)}) copy-start(bf16[128,3072]{1,0:T(8,128)(2,1)} %param.31) | copy-start | bytes 2359300
  162.4 13.0 %collective-permute-start.3 = (bf16[1024,256]{1,0:T(8,128)(2,1)S(1)}, bf16[1024,256]{1,0:T(8,128)(2,1)S(1)}, u32[]{:S(2)}, u32[]{:S(2)}) collective-permute-start(bf16[1024,256]{1,0:T(8,128)(2,1)S(1)} %pad_maximum_fusion.2), channel_id=1, source_target_pairs={{0,2},{1,3},{4,6},{5,7},{8,10},{9,11},{12,14},{13,15},{16,18},{17,... | collective-permute-start | bytes 1572872 | tf_op jit(solution)/shard_map/ppermute | solution.py:862
  164.1 22.7 %collective-permute-start.1 = (bf16[256,1024]{1,0:T(8,128)(2,1)}, bf16[256,1024]{1,0:T(8,128)(2,1)}, u32[]{:S(2)}, u32[]{:S(2)}) collective-permute-start(bf16[256,1024]{1,0:T(8,128)(2,1)} %output0_ref.1), channel_id=1, source_target_pairs={{0,2},{1,3},{2,0},{3,1},{4,6},{5,7},{6,4},{7,5},{8,10},{9,11},{10,... | collective-permute-start | bytes 1572872 | tf_op jit(solution)/shard_map/ppermute | solution.py:835
  199.1 28.9 %collective-permute-start.2 = (bf16[1024,256]{1,0:T(8,128)(2,1)S(1)}, bf16[1024,256]{1,0:T(8,128)(2,1)S(1)}, u32[]{:S(2)}, u32[]{:S(2)}) collective-permute-start(bf16[1024,256]{1,0:T(8,128)(2,1)S(1)} %pad_maximum_fusion.1), channel_id=1, source_target_pairs={{0,2},{1,3},{4,6},{5,7},{8,10},{9,11},{12,14},{13,15},{16,18},{17,... | collective-permute-start | bytes 1572872 | tf_op jit(solution)/shard_map/ppermute | solution.py:867
  223.6 27.5 %collective-permute-start.4 = (bf16[1024,256]{1,0:T(8,128)(2,1)S(1)}, bf16[1024,256]{1,0:T(8,128)(2,1)S(1)}, u32[]{:S(2)}, u32[]{:S(2)}) collective-permute-start(bf16[1024,256]{1,0:T(8,128)(2,1)S(1)} %pad_maximum_fusion.3), channel_id=1, source_target_pairs={{2,0},{3,1},{6,4},{7,5},{10,8},{11,9},{14,12},{15,13},{18,16},{19,... | collective-permute-start | bytes 1572872 | tf_op jit(solution)/shard_map/ppermute | solution.py:872
  225.1 138.5 %collective-permute-start.6 = (bf16[1024,1024]{1,0:T(8,128)(2,1)}, bf16[1024,1024]{1,0:T(8,128)(2,1)}, u32[]{:S(2)}, u32[]{:S(2)}) collective-permute-start(bf16[1024,1024]{1,0:T(8,128)(2,1)} %up_ref.1), channel_id=1, source_target_pairs={{0,2},{1,3},{2,0},{3,1},{4,6},{5,7},{6,4},{7,5},{8,10},{9,11},{10,... | collective-permute-start | bytes 6291464 | tf_op jit(solution)/shard_map/ppermute | solution.py:839
  228.0 135.6 %collective-permute-start.7 = (bf16[1024,1024]{1,0:T(8,128)(2,1)}, bf16[1024,1024]{1,0:T(8,128)(2,1)}, u32[]{:S(2)}, u32[]{:S(2)}) collective-permute-start(bf16[1024,1024]{1,0:T(8,128)(2,1)} %down_ref.1), channel_id=1, source_target_pairs={{0,2},{1,3},{2,0},{3,1},{4,6},{5,7},{6,4},{7,5},{8,10},{9,11},{10,... | collective-permute-start | bytes 6291464 | tf_op jit(solution)/shard_map/ppermute | solution.py:840
  249.0 91.3 %collective-permute-start.5 = (bf16[1024,256]{1,0:T(8,128)(2,1)S(1)}, bf16[1024,256]{1,0:T(8,128)(2,1)S(1)}, u32[]{:S(2)}, u32[]{:S(2)}) collective-permute-start(bf16[1024,256]{1,0:T(8,128)(2,1)S(1)} %pad_maximum_fusion.4), channel_id=1, source_target_pairs={{2,0},{3,1},{6,4},{7,5},{10,8},{11,9},{14,12},{15,13},{18,16},{19,... | collective-permute-start | bytes 1572872 | tf_op jit(solution)/shard_map/ppermute | solution.py:876
  362.2 40.2 %collective-permute-start.9 = (bf16[768,1024]{1,0:T(8,128)(2,1)}, bf16[768,1024]{1,0:T(8,128)(2,1)}, u32[]{:S(2)}, u32[]{:S(2)}) collective-permute-start(bf16[768,1024]{1,0:T(8,128)(2,1)} %get-tuple-element.117), channel_id=1, source_target_pairs={{0,1},{1,0},{2,3},{3,2},{4,5},{5,4},{6,7},{7,6},{8,9},{9,8},{10,11... | collective-permute-start | bytes 4718600 | tf_op jit(solution)/shard_map/ppermute | solution.py:897
  363.6 30.1 %copy-start.11 = (f32[128,1024]{1,0:T(8,128)S(1)}, f32[128,1024]{1,0:T(8,128)}, u32[]{:S(2)}) copy-start(f32[128,1024]{1,0:T(8,128)} %get-tuple-element.133) | copy-start | bytes 1572868
  393.1 9.3 %collective-permute-start.10 = (bf16[768,1024]{1,0:T(8,128)(2,1)}, bf16[768,1024]{1,0:T(8,128)(2,1)}, u32[]{:S(2)}, u32[]{:S(2)}) collective-permute-start(bf16[768,1024]{1,0:T(8,128)(2,1)} %get-tuple-element.118), channel_id=1, source_target_pairs={{0,1},{1,0},{2,3},{3,2},{4,5},{5,4},{6,7},{7,6},{8,9},{9,8},{10,11... | collective-permute-start | bytes 4718600 | tf_op jit(solution)/shard_map/ppermute | solution.py:897
  393.2 9.2 %collective-permute-start.8 = (bf16[768,1024]{1,0:T(8,128)(2,1)}, bf16[768,1024]{1,0:T(8,128)(2,1)}, u32[]{:S(2)}, u32[]{:S(2)}) collective-permute-start(bf16[768,1024]{1,0:T(8,128)(2,1)} %get-tuple-element.116), channel_id=1, source_target_pairs={{0,1},{1,0},{2,3},{3,2},{4,5},{5,4},{6,7},{7,6},{8,9},{9,8},{10,11... | collective-permute-start | bytes 4718600 | tf_op jit(solution)/shard_map/ppermute | solution.py:897
  397.2 5.2 collective-permute-start.11
  399.6 2.8 collective-permute-start.12
  400.1 13.3 %copy-start.4 = (bf16[128,4096]{0,1:T(8,128)(2,1)}, bf16[128,4096]{0,1:T(8,128)(2,1)S(1)}, u32[]{:S(2)}) copy-start(bf16[128,4096]{0,1:T(8,128)(2,1)S(1)} %constant_dynamic-update-slice_fusion) | copy-start | bytes 3145732
  400.2 13.2 %copy-start.3 = (bf16[128,4096]{0,1:T(8,128)(2,1)}, bf16[128,4096]{0,1:T(8,128)(2,1)S(1)}, u32[]{:S(2)}) copy-start(bf16[128,4096]{0,1:T(8,128)(2,1)S(1)} %constant_dynamic-update-slice_fusion.2) | copy-start | bytes 3145732
  (21 other events, 37.1 us)
Sparse Core Ops, SparseCore 0:
  417.1 147.2 all-reduce.2
